TPU v7x, 128 devices: a whole 4x4x4 slice. The times are simulated.
128 devices in a mesh: band: 8 (over z, core), lev: 16 (over x, y).
Axes of the slice: x: 4, y: 4, z: 4, core: 2. Of those that a mesh axis runs over, the one named last changes fastest.
Arguments:
- spectral_in: bfloat16 [64, 640, 2, 1281], P('lev', 'band'), may hold values from -4 to 4
- legendre: bfloat16 [640, 128, 1281], P('band', 'lev'), may hold values from -0.15625 to 0.15625
- weights: float32 [128], P('lev'), may hold values from 0.5 to 2
- pair_order: int32 [640], replicated, may hold values from 0 to 639, each once
- row_lat: int32 [128], replicated, may hold values from 0 to 127, each once
- lon_count: int32 [128], replicated, may hold values from 20 to 5136, as said below
Outputs:
- grid_field: float32 [64, 128, 5136], P(None, ('lev', 'band'))
- spectral_out: float32 [64, 640, 2, 1281], P('lev', 'band')
Inputs may be any that keep to these rules, and one draw needn't show every extreme that they name: Row i of spectral_in, legendre and spectral_out holds wavenumbers pair_order[i] and 1279 - pair_order[i]; every value appears once. Row r of grid_field and of legendre's second dimension and weights lies on latitude row_lat[r]; every value appears once. `lon_count`: each count is 4 i + 16 for a whole number i of 1 to 1280; some latitude has 5136 longitudes and some has 20.
All inputs are finite; a program needn't handle non-finite values.
Results may differ from a plain program's by a relative error of at most 0.013.
Values may be sent and summed in bfloat16 or wider, within the bound.
No kernel may reach another device: no remote copies, remote signals or barrier semaphores. Data moves between devices by JAX's collectives and lax.ppermute only.
A program may use at most 384 MiB of HBM per device.

v0:
```python
import math

import jax
import jax.numpy as jnp
from jax import lax
from jax.sharding import PartitionSpec as P

TRUNC = 1279


two_pi = 2.0 * math.pi


def wave_basis(waves, count):
    width = 4 * TRUNC + 20
    blocks = (width + 127) // 128
    coarse = jnp.arange(blocks, dtype=jnp.int32) * 128
    fine = jnp.arange(128, dtype=jnp.int32)
    scale = two_pi / count.astype(jnp.float32)
    alpha = scale * (waves[:, :, None] * coarse[None, None, :] % count).astype(jnp.float32)
    beta = scale * (waves[:, :, None] * fine[None, None, :] % count).astype(jnp.float32)
    cos_a = jnp.cos(alpha)[:, :, :, None]
    sin_a = jnp.sin(alpha)[:, :, :, None]
    cos_b = jnp.cos(beta)[:, :, None, :]
    sin_b = jnp.sin(beta)[:, :, None, :]
    shape = (2, waves.shape[1], blocks * 128)
    cos_full = (cos_a * cos_b - sin_a * sin_b).reshape(shape)[:, :, :width]
    sin_full = (sin_a * cos_b + cos_a * sin_b).reshape(shape)[:, :, :width]
    longitude = jnp.arange(width, dtype=jnp.int32)
    active = (2 * waves[:, :, None] < count) & (longitude[None, None, :] < count)
    kappa = jnp.where(waves == 0, 1.0, 2.0).astype(jnp.float32)
    factor = kappa / jnp.sqrt(count.astype(jnp.float32))
    cosine = jnp.where(active, factor[:, :, None] * cos_full, 0.0)
    sine = jnp.where(active, -factor[:, :, None] * sin_full, 0.0)
    table = jnp.stack([cosine, sine], axis=1)
    table = table.reshape(4 * waves.shape[1], width).astype(jnp.bfloat16)
    return (table, kappa)


def row_step(fourier_row, count, weight, waves):
    table, kappa = wave_basis(waves, count)
    levels = fourier_row.shape[1]
    pairs = fourier_row.shape[2]
    coeffs = jnp.transpose(fourier_row, (1, 0, 2)).reshape(levels, 4 * pairs)
    grid_row = jnp.dot(coeffs, table, preferred_element_type=jnp.float32)
    product = (grid_row * jnp.roll(grid_row, -1, axis=0)).astype(jnp.bfloat16)
    raw = lax.dot_general(
        product, table, (((1,), (1,)), ((), ())), preferred_element_type=jnp.float32
    )
    scale = weight / kappa
    scale_full = jnp.broadcast_to(scale[:, None, :], (2, 2, pairs)).reshape(4 * pairs)
    back = (raw * scale_full[None, :]).astype(jnp.bfloat16).reshape(levels, 4, pairs)
    return (grid_row, jnp.transpose(back, (1, 0, 2)))


def invert(table, spectra, masks):
    pair_rows, row_count, coefs = table.shape
    field_count = spectra.shape[0]
    masked = jnp.where(masks[:, None, :, None, :], spectra[None], jnp.zeros((), spectra.dtype))
    masked = jnp.transpose(masked, (2, 4, 0, 3, 1)).reshape(pair_rows, coefs, 4 * field_count)
    summed = jnp.einsum("prk,pkj->prj", table, masked, preferred_element_type=jnp.float32)
    summed = summed.reshape(pair_rows, row_count, 4, field_count)
    return jnp.transpose(summed, (1, 2, 3, 0)).astype(jnp.bfloat16)


def contract(table, part):
    pair_rows, row_count, coefs = table.shape
    right_side = jnp.transpose(part, (3, 0, 1, 2)).reshape(pair_rows, row_count, -1)
    return jnp.einsum("prk,prj->pjk", table, right_side, preferred_element_type=jnp.float32)


def combine(summed, masks, field_count):
    pair_rows = summed.shape[0]
    coefs = summed.shape[2]
    split_up = summed.reshape(pair_rows, 2, 2, field_count, coefs)
    result = jnp.where(masks[0][:, None, None, :], split_up[:, 0], 0.0) + jnp.where(
        masks[1][:, None, None, :], split_up[:, 1], 0.0
    )
    return jnp.transpose(result, (2, 0, 1, 3))


def shards(spectral_in, legendre, weights, pair_order, row_lat, lon_count):
    band_count = lax.axis_size("band")
    lev_count = lax.axis_size("lev")
    band_place = lax.axis_index("band")
    lev_place = lax.axis_index("lev")
    pairs_dev, lat_dev, coefs = legendre.shape
    rows_grid = lat_dev // band_count
    levels_dev = spectral_in.shape[0]
    levels = levels_dev * lev_count
    all_pairs = pair_order.shape[0]
    my_orders = lax.dynamic_slice_in_dim(pair_order, band_place * pairs_dev, pairs_dev)
    slot_index = jnp.arange(coefs, dtype=jnp.int32)
    first_slot = slot_index[None, :] < (TRUNC + 1 - my_orders)[:, None]
    masks = jnp.stack([first_slot, jnp.logical_not(first_slot)], 0)
    waves = jnp.stack([pair_order, TRUNC - pair_order], 0)
    row_base = (lev_place * band_count + band_place) * rows_grid
    my_rows = lax.dynamic_slice_in_dim(row_lat, row_base, rows_grid)
    latitudes = jnp.arange(lon_count.shape[0], dtype=jnp.int32)
    my_counts = jnp.sum(
        jnp.where(my_rows[:, None] == latitudes[None, :], lon_count[None, :], 0), axis=1
    )
    my_weights = lax.dynamic_slice_in_dim(weights, band_place * rows_grid, rows_grid)
    fourier = invert(lax.all_gather(legendre, "lev", axis=1, tiled=True), spectral_in, masks)
    fourier = fourier.reshape(lev_count, band_count, rows_grid, 4, levels_dev, pairs_dev)
    fourier = lax.all_to_all(
        lax.all_to_all(fourier, "band", split_axis=1, concat_axis=5, tiled=True),
        "lev",
        split_axis=0,
        concat_axis=4,
        tiled=True,
    )
    fourier = fourier.reshape(rows_grid, 4, levels, all_pairs)

    def grid_step(carry, item):
        row_data, count, weight = item
        grid_row, back = row_step(row_data, count, weight, waves)
        return (carry, (grid_row, back))

    unused, (grid_rows, returned) = lax.scan(grid_step, 0, (fourier, my_counts, my_weights))
    grid_field = jnp.transpose(grid_rows, (1, 0, 2))
    back = returned.reshape(1, 1, rows_grid, 4, levels, all_pairs)
    back = lax.all_to_all(
        lax.all_to_all(back, "band", split_axis=5, concat_axis=1, tiled=True),
        "lev",
        split_axis=4,
        concat_axis=0,
        tiled=True,
    )
    back = back.reshape(lev_count * lat_dev, 4, levels_dev, pairs_dev)
    summed = contract(lax.all_gather(legendre, "lev", axis=1, tiled=True), back)
    spectral_out = combine(summed, masks, levels_dev)
    return (grid_field, spectral_out)


def solution(mesh):
    return jax.shard_map(
        shards,
        mesh=mesh,
        in_specs=(P("lev", "band", None, None), P("band", "lev", None), P("lev"), P(), P(), P()),
        out_specs=(P(None, ("lev", "band"), None), P("lev", "band", None, None)),
        check_vma=False,
    )
```

profile of v0, /device:TPU:0, one launch (start us, length us, event | category | flops | bytes accessed | tf_op | source)
XLA Modules:
  0.0 391.6 jit_solution(2649393176654085227)
XLA Ops:
  9.1 2.0 fusion.28
  14.7 2.4 copy.46
  19.8 4.2 %broadcast_select_fusion = bf16[80,1281,2,2,4]{1,4,3,2,0:T(4,128)(2,1)} fusion(pred[80,1281,2]{1,2,0:T(4,128)(4,1)S(1)} %add_bitcast_fusion, bf16[80,1281,2,4]{1,3,2,0:T(4,128)(2,1)S(1)} %copy.46), kind=kLoop, calls=%fused_computation.15 | loop fusion | flops 1639680 | bytes 5124000 | tf_op jit(solution)/shard_map/jit(_where)/select_n | solution.py:59
  24.0 7.2 %select_n.89 = bf16[80,1281,16]{1,2,0:T(8,128)(2,1)} reshape(bf16[80,1281,2,2,4]{1,4,3,2,0:T(4,128)(2,1)} %broadcast_select_fusion) | data formatting | bytes 6558720 | tf_op jit(solution)/shard_map/jit(_where)/select_n | solution.py:59
  33.9 3.3 fusion.22
  37.2 8.8 %fusion.14 = (f32[2,640,128]{1,2,0:T(8,128)S(1)}, f32[2,640,128]{1,2,0:T(8,128)S(1)}) fusion(s32[]{:T(128)S(6)} %select_n.93, s32[2,640]{1,0:T(2,128)S(1)} %pad_add_fusion, f32[]{:T(128)S(6)} %div.33, pred[]{:T(512)S(6)} %lt.114), kind=kLoop, calls=%fused_computation.29 | loop fusion | flops 1638400 | bytes 1315849 | tf_op jit(solution)/shard_map/while/body/eval_jaxpr/cos | solution.py:24
  46.1 18.1 %multiply_subtract_fusion = (f32[2,640,41,128]{1,3,2,0:T(8,128)}, f32[2,640,41,128]{1,3,2,0:T(8,128)}) fusion(f32[2,640,128]{1,2,0:T(8,128)S(1)} %get-tuple-element.45, f32[2,640,41]{1,2,0:T(8,128)S(1)} %get-tuple-element.42, f32[2,640,128]{1,2,0:T(8,128)S(1)} %get-tuple-element.44, f32[2,640,41]{1,2,0:T(8,128)S(1)} %get-tuple-element.41), kind=kLoop, calls=%fused_computation.4 | loop fusion | flops 40304640 | bytes 55470080 | tf_op jit(solution)/shard_map/while/body/eval_jaxpr/sub | solution.py:27
  64.1 121.4 %all-gather.2.cloned.1.call-done = bf16[80,128,1281]{2,1,0:T(8,128)(2,1)} async-done(((bf16[80,8,1281]{2,1,0:T(8,128)(2,1)}), bf16[80,128,1281]{2,1,0:T(8,128)(2,1)}) %all-gather.2.cloned.1.call-update) | async-done | bytes 26234896 | tf_op jit(solution)/shard_map/all_gather | solution.py:104
  185.5 13.8 %convolution_convert_fusion = bf16[80,16,128]{2,1,0:T(8,128)(2,1)S(1)} fusion(bf16[80,1281,16]{1,2,0:T(8,128)(2,1)} %select_n.89, bf16[80,128,1281]{2,1,0:T(8,128)(2,1)} %all-gather.2.cloned.1.call-done), kind=kOutput, calls=%fused_computation.21 | convolution fusion | flops 419921920 | bytes 29841920 | tf_op jit(solution)/shard_map/prk,pkj->prj/dot_general | solution.py:61
  200.6 4.4 %all-to-all-start = ((bf16[16,8,1,4,4,80]{5,0,4,3,2,1:T(8,128)(2,1)}), bf16[16,8,1,4,4,80]{5,0,4,3,2,1:T(8,128)(2,1)S(1)}, u32[]{:S(2)}, u32[]{:S(2)}) async-start(bf16[16,8,1,4,4,80]{5,0,4,3,2,1:T(8,128)(2,1)} %copy.48), calls=%async_computation | async-start | bytes 1048576 | tf_op jit(solution)/shard_map/all_to_all | solution.py:107
  205.0 27.4 %fusion = (bf16[2,1,640,5136]{2,3,0,1:T(8,128)(2,1)}, bf16[2,1,640,5136]{2,3,0,1:T(8,128)(2,1)}) fusion(f32[2,640,5248]{1,2,0:T(8,128)} %bitcast.81, f32[2,640]{1,0:T(2,128)S(1)} %get-tuple-element.34, pred[2,640]{1,0:T(4,128)(4,1)S(1)} %multiply_compare_fusion, pred[5136]{0:T(1024)(128)(4,1)S(1)} %iota_compare_fusion.2, f32[2,640,5248]{1,2,0:T(8,128)} %bitcast.82, ...), kind=kLoop, calls=%fused_computation.5 | loop fusion | flops 32870400 | bytes 78905616 | tf_op jit(solution)/shard_map/while/body/eval_jaxpr/stack | solution.py:35
  234.0 5.3 %all-to-all-start.1 = ((bf16[16,1,1,4,4,640]{5,4,3,2,1,0:T(4,128)(2,1)}), bf16[16,1,1,4,4,640]{5,4,3,2,1,0:T(4,128)(2,1)S(1)}, u32[]{:S(2)}, u32[]{:S(2)}) async-start(bf16[16,1,1,4,4,640]{5,4,3,2,1,0:T(4,128)(2,1)} %reshape.277), calls=%async_computation.1 | async-start | bytes 655360 | tf_op jit(solution)/shard_map/all_to_all | solution.py:106
  239.3 18.3 %maximum_convert_fusion = bf16[2,2,640,5136]{2,3,0,1:T(8,128)(2,1)} fusion(bf16[2,1,640,5136]{2,3,0,1:T(8,128)(2,1)} %get-tuple-element.40, bf16[2,1,640,5136]{2,3,0,1:T(8,128)(2,1)} %get-tuple-element.39), kind=kLoop, calls=%fused_computation | loop fusion | flops 13148160 | bytes 52592640 | tf_op jit(solution)/shard_map/while/body/eval_jaxpr/convert_element_type | solution.py:36
  257.6 33.2 %copy.52 = bf16[2,2,640,5136]{3,2,1,0:T(8,128)(2,1)} copy(bf16[2,2,640,5136]{2,3,0,1:T(8,128)(2,1)} %maximum_convert_fusion) | data formatting | bytes 52592640 | tf_op jit(solution)/shard_map/while/body/eval_jaxpr/convert_element_type | solution.py:36
  291.1 11.1 %fusion.34 = f32[64,5136]{1,0:T(8,128)S(1)} fusion(bf16[64,2560]{1,0:T(8,128)(2,1)S(1)} %bitcast.92, bf16[2560,5136]{1,0:T(8,128)(2,1)} %bitcast.79), kind=kOutput, calls=%fused_computation.62 | convolution fusion | flops 1682964480 | bytes 27938816 | tf_op jit(solution)/shard_map/while/body/eval_jaxpr/dot_general | solution.py:45
  302.3 13.5 %fusion.6 = bf16[64,2560]{1,0:T(8,128)(2,1)S(1)} fusion(bf16[2560,5136]{1,0:T(8,128)(2,1)} %bitcast.80, f32[64,5136]{1,0:T(8,128)S(1)} %fusion.34, f32[1,5136]{1,0:T(1,128)S(1)} %slice.33, f32[63,5136]{1,0:T(8,128)S(1)} %slice.32, f32[2560]{0:T(1024)S(1)} %mul.242), kind=kOutput, calls=%fused_computation.17 | convolution fusion | flops 1684278272 | bytes 29263872 | tf_op jit(solution)/shard_map/while/body/eval_jaxpr/dot_general | solution.py:47
  317.6 13.1 %all_to_all.66 = bf16[8,2,10240]{2,1,0:T(2,128)(2,1)S(1)} all-to-all(bf16[8,2,10240]{2,1,0:T(2,128)(2,1)S(1)} %reshape.278), channel_id=1, replica_groups=mesh['band'=8,'lev'=16] {'band'}, dimensions={0} | all-to-all | bytes 655360 | tf_op jit(solution)/shard_map/all_to_all | solution.py:124
  332.7 7.2 %all-to-all-start.3 = ((bf16[1,8,1,4,64,80]{5,1,3,2,0,4:T(8,128)(2,1)}), bf16[1,8,1,4,64,80]{5,1,3,2,0,4:T(8,128)(2,1)S(1)}, u32[]{:S(2)}, u32[]{:S(2)}) async-start(bf16[1,8,1,4,64,80]{5,1,3,2,0,4:T(8,128)(2,1)} %bitcast.24), calls=%async_computation.3 | async-start | bytes 1048576 | tf_op jit(solution)/shard_map/all_to_all | solution.py:123
  340.1 2.4 copy.60
  342.5 8.8 %all-to-all-done.3 = bf16[1,8,1,4,64,80]{5,1,3,2,0,4:T(8,128)(2,1)S(1)} async-done(((bf16[1,8,1,4,64,80]{5,1,3,2,0,4:T(8,128)(2,1)}), bf16[1,8,1,4,64,80]{5,1,3,2,0,4:T(8,128)(2,1)S(1)}, u32[]{:S(2)}, u32[]{:S(2)}) %all-to-all-start.3) | async-done | bytes 327712 | tf_op jit(solution)/shard_map/all_to_all | solution.py:123
  351.9 14.5 %fusion.35 = f32[80,16,1281]{2,1,0:T(8,128)} fusion(bf16[80,128,16]{1,2,0:T(8,128)(2,1)S(1)} %bitcast.91, bf16[80,128,1281]{2,1,0:T(8,128)(2,1)} %all-gather.2.cloned.1.call-done), kind=kOutput, calls=%fused_computation.63 | convolution fusion | flops 419758080 | bytes 33121280 | tf_op jit(solution)/shard_map/prk,prj->pjk/dot_general | solution.py:69
  366.3 9.1 %reshape.276 = f32[80,2,2,4,1281]{4,3,2,1,0:T(4,128)} reshape(f32[80,16,1281]{2,1,0:T(8,128)} %fusion.35) | data formatting | bytes 13117440 | tf_op jit(solution)/shard_map/reshape | solution.py:75
  375.4 4.4 %fusion.33 = (f32[80,1,2,4,1281]{4,3,2,1,0:T(4,128)S(1)}, f32[80,1,2,4,1281]{4,3,2,1,0:T(4,128)S(1)}) fusion(f32[80,2,2,4,1281]{4,3,2,1,0:T(4,128)} %reshape.276), kind=kLoop, calls=%fused_computation.60 | loop fusion | bytes 13117440 | tf_op jit(solution)/shard_map/slice | solution.py:76
  379.8 4.6 %fusion.4 = f32[4,80,2,1281]{3,2,1,0:T(2,128)} fusion(f32[80,1,2,4,1281]{4,3,2,1,0:T(4,128)S(1)} %get-tuple-element.36, f32[80,1,2,4,1281]{4,3,2,1,0:T(4,128)S(1)} %get-tuple-element.35, pred[80,1281]{1,0:T(8,128)(4,1)S(1)} %get-tuple-element.47, pred[80,1281]{1,0:T(8,128)(4,1)S(1)} %get-tuple-element.46), kind=kLoop, calls=%fused_computation.12 | loop fusion | flops 2459520 | bytes 10043040 | tf_op jit(solution)/shard_map/transpose | solution.py:79
  (39 shorter events, 16.3 us)
Async XLA Ops:
  7.2 178.3 %all-gather.2.cloned.1.call-start = ((), (), s32[]{:S(2)}) async-start(), calls=%async_computation.4 | async-start | bytes 30638080 | tf_op jit(solution)/shard_map/all_gather | solution.py:104
  18.7 12.5 %copy-start = (f32[8]{0:T(128)S(1)}, f32[8]{0:T(128)}, u32[]{:S(2)}) copy-start(f32[8]{0:T(128)} %param.8) | copy-start | bytes 100
  200.6 31.8 %all-to-all-start = ((bf16[16,8,1,4,4,80]{5,0,4,3,2,1:T(8,128)(2,1)}), bf16[16,8,1,4,4,80]{5,0,4,3,2,1:T(8,128)(2,1)S(1)}, u32[]{:S(2)}, u32[]{:S(2)}) async-start(bf16[16,8,1,4,4,80]{5,0,4,3,2,1:T(8,128)(2,1)} %copy.48), calls=%async_computation | async-start | bytes 1048576 | tf_op jit(solution)/shard_map/all_to_all | solution.py:107
  234.0 56.8 %all-to-all-start.1 = ((bf16[16,1,1,4,4,640]{5,4,3,2,1,0:T(4,128)(2,1)}), bf16[16,1,1,4,4,640]{5,4,3,2,1,0:T(4,128)(2,1)S(1)}, u32[]{:S(2)}, u32[]{:S(2)}) async-start(bf16[16,1,1,4,4,640]{5,4,3,2,1,0:T(4,128)(2,1)} %reshape.277), calls=%async_computation.1 | async-start | bytes 655360 | tf_op jit(solution)/shard_map/all_to_all | solution.py:106
  332.7 18.6 %all-to-all-start.3 = ((bf16[1,8,1,4,64,80]{5,1,3,2,0,4:T(8,128)(2,1)}), bf16[1,8,1,4,64,80]{5,1,3,2,0,4:T(8,128)(2,1)S(1)}, u32[]{:S(2)}, u32[]{:S(2)}) async-start(bf16[1,8,1,4,64,80]{5,1,3,2,0,4:T(8,128)(2,1)} %bitcast.24), calls=%async_computation.3 | async-start | bytes 1048576 | tf_op jit(solution)/shard_map/all_to_all | solution.py:123
Sparse Core Ops, SparseCore 0:
  10.2 175.2 all-gather.1
where the time goes:
time: 398 us; the launch traced here: 392 us
  waiting for transfers between devices  131 us (33%)
  other arithmetic  92.4 us (23%)
  local copies, waits for them, and re-layouts  68.6 us (17%)
  matrix products  52.9 us (13%)
  starting transfers between devices  17 us (4%)
  between operations  16.8 us (4%)
  blocking collectives  13.1 us (3%)
    all_gather x1, waiting for transfers between devices, shards(): lax.all_gather(legendre, 'lev', axis=1, tiled=True)  121 us
    convert_element_type x1, local copies, waits for them, and re-layouts, wave_basis(): table = table.reshape(4 * waves.shape[1], width).astype(jnp.bfloat16)  33.2 us
    another operation x1, other arithmetic, wave_basis(): table = jnp.stack([cosine, sine], axis=1)  27.4 us
    convert_element_type x1, other arithmetic, wave_basis(): table = table.reshape(4 * waves.shape[1], width).astype(jnp.bfloat16)  18.3 us
    sub x1, other arithmetic, wave_basis(): cos_full = (cos_a * cos_b - sin_a * sin_b).reshape(shape)[:, :, :width]  18.1 us
    dot_general x1, matrix products, contract(): jnp.einsum('prk,prj->pjk', table, right_side, preferred_element_type=jnp....  14.5 us
    dot_general x1, matrix products, invert(): jnp.einsum('prk,pkj->prj', table, masked, preferred_element_type=jnp.floa...  13.8 us
    dot_general x1, matrix products, row_step(): lax.dot_general(product, table, (((1,), (1,)), ((), ())), preferred_eleme...  13.5 us
  transfers between devices with their start and end apart: 4, of which 2 were waited for; matrix products, arithmetic and copies ran while one was open for 35% of the time, Pallas kernels for 0%

commit v1 on v0

v1 whole, which is shorter than its diff:
```python
import functools
import math

import jax
import jax.numpy as jnp
from jax import lax
from jax.experimental import pallas as pl
from jax.experimental.pallas import tpu as pltpu
from jax.sharding import PartitionSpec as P

TRUNC = 1279
COEFS = TRUNC + 2
LANES = 128
BLOCKS = (COEFS - 1) // LANES
QUARTER = 11
WIDTH = 4 * TRUNC + 20

f32 = jnp.float32
bf16 = jnp.bfloat16

NT = (((1,), (1,)), ((), ()))


def params(mib=48):
    return pltpu.CompilerParams(vmem_limit_bytes=mib * 1024 * 1024)


def pack_kernel(leg_ref, spec_ref, out_ref):
    pairs = leg_ref.shape[0]
    lane = lax.broadcasted_iota(jnp.int32, (16, LANES), 1)
    tail = jnp.zeros((16, LANES), f32)
    for p in range(pairs):
        table = leg_ref[p].astype(f32)
        spec = jnp.concatenate([spec_ref[l, p].astype(f32) for l in range(4)], axis=0)
        rows = jnp.concatenate([table, spec], axis=0)
        for b in range(BLOCKS):
            out_ref[0, p * BLOCKS + b] = rows[:, b * LANES : (b + 1) * LANES].astype(bf16)
        tail = jnp.where(lane == p, rows[:, COEFS - 1 : COEFS], tail)
    out_ref[0, pairs * BLOCKS] = tail.astype(bf16)


def pack(legendre, spectral):
    pairs_dev = legendre.shape[0]
    pairs = pairs_dev // 16
    return pl.pallas_call(
        pack_kernel,
        grid=(16,),
        in_specs=[
            pl.BlockSpec((pairs, 8, COEFS), lambda d: (d, 0, 0)),
            pl.BlockSpec((4, pairs, 2, COEFS), lambda d: (0, d, 0, 0)),
        ],
        out_specs=pl.BlockSpec((1, pairs * BLOCKS + 1, 16, LANES), lambda d: (d, 0, 0, 0)),
        out_shape=jax.ShapeDtypeStruct((16, pairs * BLOCKS + 1, 16, LANES), bf16),
        compiler_params=params(),
        name="pack",
    )(legendre, spectral)


def gathered(main_ref, tail_ref):
    blocks = [main_ref[:, b].reshape(256, LANES) for b in range(BLOCKS)]
    blocks.append(tail_ref[:, 0].reshape(256, LANES))
    return jnp.concatenate(blocks, axis=1)


def invert_kernel(split_ref, main_ref, tail_ref, pick_ref, out_ref):
    p = pl.program_id(0)
    split = split_ref[p]
    data = gathered(main_ref, tail_ref)
    slot = lax.broadcasted_iota(jnp.int32, (16, data.shape[1]), 1)
    whole = BLOCKS * LANES
    first = (slot < split) & (slot < whole)
    second = ((slot >= split) & (slot < whole)) | (slot == whole + p)
    first = jnp.where(first, 1.0, 0.0).astype(bf16)
    second = jnp.where(second, 1.0, 0.0).astype(bf16)
    shape = (16, 16, data.shape[1])
    apart = data.reshape(shape)
    low = (apart * first[None]).reshape(data.shape)
    high = (apart * second[None]).reshape(data.shape)
    for s, part in enumerate((low, high)):
        full = lax.dot_general(data, part, NT, preferred_element_type=f32)
        rows = full.reshape(16, 16, 256)[:, :8].reshape(128, 256).astype(bf16)
        out_ref[0, s] = jnp.dot(rows, pick_ref[...], preferred_element_type=f32).astype(bf16)


def invert(splits, buffer, pick):
    pairs = splits.shape[0]
    return pl.pallas_call(
        invert_kernel,
        grid=(pairs,),
        in_specs=[
            pl.BlockSpec(memory_space=pltpu.SMEM),
            pl.BlockSpec((16, BLOCKS, 16, LANES), lambda p: (0, p, 0, 0)),
            pl.BlockSpec((16, 1, 16, LANES), lambda p: (0, pairs * BLOCKS, 0, 0)),
            pl.BlockSpec((256, LANES), lambda p: (0, 0)),
        ],
        out_specs=pl.BlockSpec((1, 2, 128, LANES), lambda p: (p, 0, 0, 0)),
        out_shape=jax.ShapeDtypeStruct((pairs, 2, 128, LANES), bf16),
        compiler_params=params(),
        name="invert",
    )(splits, buffer, buffer, pick)


def contract_kernel(split_ref, main_ref, tail_ref, order_ref, spread_ref, back_ref, out_ref):
    p = pl.program_id(0)
    split = split_ref[p]
    data = gathered(main_ref, tail_ref)
    sums = []
    for s in range(2):
        turned = lax.dot_general(order_ref[...], back_ref[0, s], NT, preferred_element_type=f32)
        spread = jnp.dot(turned.astype(bf16), spread_ref[...], preferred_element_type=f32)
        sums.append(jnp.dot(spread.astype(bf16), data, preferred_element_type=f32))
    slot = lax.broadcasted_iota(jnp.int32, sums[0].shape, 1)
    result = jnp.where(slot < split, sums[0], sums[1])
    for b in range(0, BLOCKS, 2):
        left = result[:, b * LANES : (b + 1) * LANES].reshape(16, 8, LANES)
        right = result[:, (b + 1) * LANES : (b + 2) * LANES].reshape(16, 8, LANES)
        both = jnp.concatenate([left, right], axis=1).astype(bf16)
        out_ref[:, pl.ds(p * (BLOCKS // 2) + b // 2, 1)] = both[:, None]
    last = sums[1][:, BLOCKS * LANES :].reshape(16, 8, LANES)
    last = jnp.concatenate([last, last], axis=1)
    lane = lax.broadcasted_iota(jnp.int32, last.shape, 2)
    end = out_ref.shape[1] - 1

    @pl.when(p == 0)
    def _():
        out_ref[:, end] = jnp.where(lane == 0, last, 0.0).astype(bf16)

    @pl.when(p > 0)
    def _():
        out_ref[:, end] = jnp.where(lane == p, last, out_ref[:, end].astype(f32)).astype(bf16)


def contract(splits, buffer, order, spread, back):
    pairs = splits.shape[0]
    out_blocks = pairs * BLOCKS // 2 + 1
    return pl.pallas_call(
        contract_kernel,
        grid=(pairs,),
        in_specs=[
            pl.BlockSpec(memory_space=pltpu.SMEM),
            pl.BlockSpec((16, BLOCKS, 16, LANES), lambda p: (0, p, 0, 0)),
            pl.BlockSpec((16, 1, 16, LANES), lambda p: (0, pairs * BLOCKS, 0, 0)),
            pl.BlockSpec((128, LANES), lambda p: (0, 0)),
            pl.BlockSpec((128, 256), lambda p: (0, 0)),
            pl.BlockSpec((1, 2, 128, LANES), lambda p: (p, 0, 0, 0)),
        ],
        out_specs=pl.BlockSpec((16, out_blocks, 16, LANES), lambda p: (0, 0, 0, 0)),
        out_shape=jax.ShapeDtypeStruct((16, out_blocks, 16, LANES), bf16),
        compiler_params=params(),
        name="contract",
    )(splits, buffer, buffer, order, spread, back)


def unpack_kernel(in_ref, out_ref):
    pairs = out_ref.shape[1]
    last = in_ref[0, in_ref.shape[1] - 1].astype(f32)
    for p in range(pairs):
        for h in range(BLOCKS // 2):
            both = in_ref[0, p * (BLOCKS // 2) + h].astype(f32)
            for side in range(2):
                b = 2 * h + side
                for l in range(4):
                    row = side * 8 + 2 * l
                    out_ref[l, p, :, b * LANES : (b + 1) * LANES] = both[row : row + 2]
        for l in range(4):
            out_ref[l, p, :, COEFS - 1 : COEFS] = last[2 * l : 2 * l + 2, p : p + 1]


def unpack(buffer, pairs):
    blocks = buffer.shape[1]
    return pl.pallas_call(
        unpack_kernel,
        grid=(16,),
        in_specs=[pl.BlockSpec((1, blocks, 16, LANES), lambda d: (d, 0, 0, 0))],
        out_specs=pl.BlockSpec((4, pairs, 2, COEFS), lambda d: (0, d, 0, 0)),
        out_shape=jax.ShapeDtypeStruct((4, 16 * pairs, 2, COEFS), f32),
        compiler_params=params(),
        name="unpack",
    )(buffer)


def turn(whole, part):
    scaled = part * (4.0 / whole)
    nearest = jnp.floor(scaled + 0.5)
    angle = (scaled - nearest) * (math.pi / 2)
    square = angle * angle
    sine = angle + angle * square * (
        -1.6666654611e-1 + square * (8.3321608736e-3 - 1.9515295891e-4 * square)
    )
    cosine = 1.0 - 0.5 * square + square * square * (
        4.166664568298827e-2 + square * (-1.388731625493765e-3 + 2.443315711809948e-5 * square)
    )
    odd = (nearest == 1.0) | (nearest == 3.0)
    cos_base = jnp.where(odd, sine, cosine)
    sin_base = jnp.where(odd, cosine, sine)
    cos_sign = jnp.where((nearest == 1.0) | (nearest == 2.0), -1.0, 1.0)
    sin_sign = jnp.where((nearest == 2.0) | (nearest == 3.0), -1.0, 1.0)
    return cos_base * cos_sign, sin_base * sin_sign


def remainder(value, whole):
    quotient = jnp.floor(value * (1.0 / whole))
    rest = value - quotient * whole
    rest = jnp.where(rest < 0.0, rest + whole, rest)
    return jnp.where(rest >= whole, rest - whole, rest)


def basis_kernel(count_ref, order_ref, out_ref):
    whole = count_ref[0].astype(f32)
    order = order_ref[...]
    even = jnp.where(order % 2 == 0, order, TRUNC - order)
    rows = order.shape[0]
    lane = lax.broadcasted_iota(jnp.int32, (rows, LANES), 1).astype(f32)
    for kind in range(2):
        wave = (even if kind == 0 else TRUNC - even).astype(f32)
        cos_fine, sin_fine = turn(whole, remainder(wave * lane, whole))
        cos_coarse, sin_coarse = turn(whole, remainder(wave * (lane * 128.0), whole))
        for a in range(QUARTER):
            cos_a = cos_coarse[:, a : a + 1]
            sin_a = sin_coarse[:, a : a + 1]
            at = pl.ds(a * LANES, LANES)
            out_ref[2 * kind, :, at] = (cos_a * cos_fine - sin_a * sin_fine).astype(bf16)
            out_ref[2 * kind + 1, :, at] = (sin_a * cos_fine + cos_a * sin_fine).astype(bf16)


def basis(count, order):
    pairs = order.shape[0]
    rows = 128
    return pl.pallas_call(
        basis_kernel,
        grid=(pairs // rows,),
        in_specs=[
            pl.BlockSpec(memory_space=pltpu.SMEM),
            pl.BlockSpec((rows, 1), lambda i: (i, 0)),
        ],
        out_specs=pl.BlockSpec((4, rows, QUARTER * LANES), lambda i: (0, i, 0)),
        out_shape=jax.ShapeDtypeStruct((4, pairs, QUARTER * LANES), bf16),
        compiler_params=params(),
        cost_estimate=pl.CostEstimate(flops=200_000_000, bytes_accessed=30_000_000, transcendentals=0),
        name="basis",
    )(count, order)


def grid_kernel(count_ref, weight_ref, order_ref, table_ref, eye_ref, in_ref, grid_ref, back_ref, place):
    count = count_ref[0]
    quarter = count // 4
    whole = jnp.full((1, LANES), count.astype(f32))
    shrink = lax.rsqrt(whole)
    order = order_ref[...]
    pairs = order.shape[0]
    is_even = order % 2 == 0
    even = jnp.where(is_even, order, TRUNC - order)
    odd = TRUNC - even
    lane = lax.broadcasted_iota(jnp.int32, (pairs, LANES), 1)
    left = lane < 64

    def column(condition, yes, no):
        return jnp.broadcast_to(jnp.where(condition, yes, no).astype(f32), (pairs, LANES))

    swap = column(is_even, 1.0, 0.0) > 0.5
    sign_even = column(even % 4 == 0, 1.0, -1.0)
    sign_odd = column(odd % 4 == 1, 1.0, -1.0)
    keep_even = column(2 * even < count, jnp.where(even == 0, 1.0, 2.0), 0.0)
    keep_odd = column(2 * odd < count, 2.0, 0.0)
    first = in_ref[0].astype(f32)
    second = in_ref[1].astype(f32)
    coef_even = jnp.where(swap, first, second) * keep_even
    coef_odd = jnp.where(swap, second, first) * keep_odd
    turned_even = pltpu.roll(coef_even, 64, 1)
    turned_odd = pltpu.roll(coef_odd, 64, 1)
    even_cos = jnp.where(left, coef_even, turned_even * sign_even)
    even_sin = -jnp.where(left, turned_even, coef_even * sign_even)
    odd_cos = jnp.where(left, coef_odd, -(coef_odd * sign_odd))
    odd_sin = -jnp.where(left, turned_odd, turned_odd * sign_odd)

    def upright(values):
        return lax.dot_general(eye_ref[...], values.astype(bf16), NT, preferred_element_type=f32).astype(bf16)

    sum_even = jnp.dot(upright(even_cos), table_ref[0], preferred_element_type=f32)
    sum_even += jnp.dot(upright(even_sin), table_ref[1], preferred_element_type=f32)
    sum_odd = jnp.dot(upright(odd_cos), table_ref[2], preferred_element_type=f32)
    sum_odd += jnp.dot(upright(odd_sin), table_ref[3], preferred_element_type=f32)

    width = QUARTER * LANES
    along = lax.broadcasted_iota(jnp.int32, (1, width), 1)
    factor = jnp.where(along < quarter, jnp.broadcast_to(shrink[:, :1], (1, width)), 0.0)
    near = (sum_even + sum_odd) * factor
    far = (sum_even - sum_odd) * factor

    place[...] = jnp.zeros_like(place)
    narrow = lax.broadcasted_iota(jnp.int32, (64, LANES), 1)
    for t, field in enumerate((near[:64], near[64:], far[:64], far[64:])):
        start = t * quarter
        shift = start % LANES
        base = start // LANES
        before = jnp.zeros((64, LANES), f32)
        for b in range(QUARTER + 1):
            if b < QUARTER:
                block = field[:, b * LANES : (b + 1) * LANES]
                block = pltpu.roll(block, shift, 1)
            else:
                block = jnp.zeros((64, LANES), f32)
            merged = jnp.where(narrow < shift, before, block)
            at = pl.ds(pl.multiple_of((base + b) * LANES, LANES), LANES)
            place[:, at] += merged
            before = block
    grid_ref[...] = place[:, :WIDTH]

    def product(field):
        return jnp.concatenate(
            [
                half * jnp.concatenate([half[1:], half[:1]], axis=0)
                for half in (field[:64], field[64:])
            ],
            axis=0,
        )

    near = product(near)
    far = product(far)
    both = (near + far).astype(bf16)
    gap = (near - far).astype(bf16)

    def analyse(index, values):
        return lax.dot_general(table_ref[index], values, NT, preferred_element_type=f32)

    x_cos = analyse(0, both)
    x_sin = analyse(1, both)
    y_cos = analyse(2, gap)
    y_sin = analyse(3, gap)
    scale = weight_ref[0] * shrink
    back_even = jnp.where(
        left,
        x_cos + sign_even * pltpu.roll(x_cos, 64, 1),
        -(sign_even * x_sin + pltpu.roll(x_sin, 64, 1)),
    )
    turned = pltpu.roll(y_sin, 64, 1)
    back_odd = jnp.where(left, y_cos - sign_odd * turned, -turned - sign_odd * y_cos)
    back_even = jnp.where(keep_even > 0.0, back_even * scale, 0.0)
    back_odd = jnp.where(keep_odd > 0.0, back_odd * scale, 0.0)
    back_ref[0] = jnp.where(swap, back_even, back_odd).astype(bf16)
    back_ref[1] = jnp.where(swap, back_odd, back_even).astype(bf16)


def grid_step(count, weight, order, table, eye, coeffs):
    pairs = order.shape[0]
    smem = pl.BlockSpec(memory_space=pltpu.SMEM)
    vmem = pl.BlockSpec(memory_space=pltpu.VMEM)
    return pl.pallas_call(
        grid_kernel,
        in_specs=[smem, smem, vmem, vmem, vmem, vmem],
        out_specs=[vmem, vmem],
        out_shape=[
            jax.ShapeDtypeStruct((64, WIDTH), f32),
            jax.ShapeDtypeStruct((2, pairs, LANES), bf16),
        ],
        scratch_shapes=[pltpu.VMEM((64, (4 * QUARTER + 2) * LANES), f32)],
        compiler_params=params(),
        name="grid",
    )(count, weight, order, table, eye, coeffs)


def shards(spectral_in, legendre, weights, pair_order, row_lat, lon_count):
    band_count = lax.axis_size("band")
    lev_count = lax.axis_size("lev")
    band_place = lax.axis_index("band")
    lev_place = lax.axis_index("lev")
    devices = band_count * lev_count
    pairs_dev = legendre.shape[0]
    pairs = pairs_dev // lev_count
    all_pairs = pair_order.shape[0]

    buffer = lax.all_to_all(pack(legendre, spectral_in), "lev", 0, 0, tiled=True)

    my_row = lax.dynamic_slice_in_dim(row_lat, lev_place * band_count + band_place, 1)
    my_count = lax.dynamic_slice_in_dim(lon_count, my_row[0], 1)
    my_weight = lax.dynamic_slice_in_dim(weights, band_place, 1)
    my_orders = lax.dynamic_slice_in_dim(pair_order, band_place * pairs_dev + lev_place * pairs, pairs)
    splits = TRUNC + 1 - my_orders
    arrived = pair_order.reshape(band_count, lev_count, pairs).transpose(2, 1, 0).reshape(all_pairs, 1)
    table = basis(my_count, arrived)

    lane = jnp.arange(LANES, dtype=jnp.int32)
    place = 16 * (lane % 64 // 4) + 8 + 2 * (lane % 4) + lane // 64
    pick = (jnp.arange(256, dtype=jnp.int32)[:, None] == place[None, :]).astype(bf16)
    order = ((lane % 2 * 64 + lane // 2)[:, None] == lane[None, :]).astype(bf16)
    spread = ((lane // 8 * 16 + lane % 8)[:, None] == jnp.arange(256, dtype=jnp.int32)[None, :]).astype(bf16)
    eye = (lane[:, None] == lane[None, :]).astype(bf16)

    fourier = invert(splits, buffer, pick)
    fourier = jnp.transpose(fourier, (2, 1, 0, 3)).reshape(devices, 2, pairs * LANES)
    fourier = lax.all_to_all(fourier, ("lev", "band"), 0, 0, tiled=True)
    fourier = fourier.reshape(devices, 2, pairs, LANES).transpose(1, 2, 0, 3).reshape(2, all_pairs, LANES)

    grid_row, back = grid_step(my_count, my_weight, arrived, table, eye, fourier)

    back = back.reshape(2, pairs, devices, LANES).transpose(2, 0, 1, 3).reshape(devices, 2, pairs * LANES)
    back = lax.all_to_all(back, ("lev", "band"), 0, 0, tiled=True)
    back = back.reshape(devices, 2, pairs, LANES).transpose(2, 1, 0, 3)

    spectral = contract(splits, buffer, order, spread, back)
    spectral = lax.all_to_all(spectral, "lev", 0, 0, tiled=True)
    return (grid_row.reshape(64, 1, WIDTH), unpack(spectral, pairs))


def solution(mesh):
    return jax.shard_map(
        shards,
        mesh=mesh,
        in_specs=(P("lev", "band", None, None), P("band", "lev", None), P("lev"), P(), P(), P()),
        out_specs=(P(None, ("lev", "band"), None), P("lev", "band", None, None)),
        check_vma=False,
    )
```

time: 398 us -> 184 us (0.46); the launches traced: 392 us -> 184 us
  other arithmetic: 92.4 us -> 0.3 us
  waiting for transfers between devices: 131 us -> 74.1 us
  matrix products: 52.9 us -> 0 us
  Pallas kernels: 0 us -> 44.8 us
  local copies, waits for them, and re-layouts: 68.6 us -> 31.3 us
  between operations: 16.8 us -> 2.71 us
  starting transfers between devices: 17 us -> 30.4 us
  blocking collectives: 13.1 us -> 0 us
    all_gather x1 -> x0, waiting for transfers between devices: 121 us -> none  [shards(): lax.all_gather(legendre, 'lev', axis=1, tiled=True)]
    all_to_all x3 -> x4, waiting for transfers between devices: 8.8 us -> 74.1 us  [the longest x1 29.1 us: shards(): lax.all_to_all(pack(legendre, spectral_in), 'lev', 0, 0, tiled=True)]
    dot_general x4 -> x0, matrix products: 52.9 us -> none  [the longest x1 14.5 us: contract(): jnp.einsum('prk,prj->pjk', table, right_side, preferred_element_type=jnp....]
    pallas_call x0 -> x6, Pallas kernels: none -> 44.8 us  [the longest x1 9.4 us: basis(): pl.pallas_call(basis_kernel, grid=(pairs // rows,), in_specs=[pl.BlockSpe...]
    convert_element_type x2 -> x0, local copies, waits for them, and re-layouts: 33.6 us -> none  [the longest x1 33.2 us: wave_basis(): table = table.reshape(4 * waves.shape[1], width).astype(jnp.bfloat16)]
    another operation x2 -> x0, other arithmetic: 27.4 us -> none  [the longest x1 27.4 us: wave_basis(): table = jnp.stack([cosine, sine], axis=1)]
    sub x3 -> x1, other arithmetic: 19.5 us -> 0.08 us  [shards(): splits = TRUNC + 1 - my_orders]
    convert_element_type x1 -> x4, other arithmetic: 18.3 us -> 0.2 us  [the longest x1 0.08 us: shards(): ((lane // 8 * 16 + lane % 8)[:, None] == jnp.arange(256, dtype=jnp.int32)...]
  transfers between devices with their start and end apart: 4 -> 4, of which waited for: 2 -> 4; matrix products, arithmetic and copies ran while one was open for 35% -> 3% of each run, Pallas kernels for 0% -> 5%
where the time goes in v1:
time: 184 us
  waiting for transfers between devices  74.1 us (40%)
  Pallas kernels  44.8 us (24%)
  local copies, waits for them, and re-layouts  31.3 us (17%)
  starting transfers between devices  30.4 us (17%)
  between operations  2.71 us (1%)
    all_to_all x1, waiting for transfers between devices, shards(): lax.all_to_all(pack(legendre, spectral_in), 'lev', 0, 0, tiled=True)  29.1 us
    all_to_all x1, waiting for transfers between devices, shards(): spectral = lax.all_to_all(spectral, 'lev', 0, 0, tiled=True)  22.6 us
    all_to_all x1, starting transfers between devices, shards(): fourier = lax.all_to_all(fourier, ('lev', 'band'), 0, 0, tiled=True)  13.6 us
    unnamed x31, local copies, waits for them, and re-layouts  13 us
    all_to_all x1, waiting for transfers between devices, shards(): fourier = lax.all_to_all(fourier, ('lev', 'band'), 0, 0, tiled=True)  11.2 us
    all_to_all x1, waiting for transfers between devices, shards(): back = lax.all_to_all(back, ('lev', 'band'), 0, 0, tiled=True)  11.2 us
    pallas_call x1, Pallas kernels, basis(): pl.pallas_call(basis_kernel, grid=(pairs // rows,), in_specs=[pl.BlockSpe...  9.4 us
    pallas_call x1, Pallas kernels, grid_step(): pl.pallas_call(grid_kernel, in_specs=[smem, smem, vmem, vmem, vmem, vmem]...  9.28 us
  transfers between devices with their start and end apart: 4, of which 4 were waited for; matrix products, arithmetic and copies ran while one was open for 3% of the time, Pallas kernels for 5%

profile of v1, /device:TPU:0, one launch (start us, length us, event | category | flops | bytes accessed | tf_op | source)
XLA Modules:
  0.0 183.5 jit_solution(3812875351560031900)
XLA Ops:
  2.1 1.5 copy-done.4
  3.6 6.5 %pack.1 = bf16[16,51,16,128]{3,2,1,0:T(8,128)(2,1)} custom-call(bf16[80,8,1281]{2,1,0:T(8,128)(2,1)S(1)} %copy-done.3, bf16[4,80,2,1281]{3,2,1,0:T(2,128)(2,1)S(1)} %copy-done.4), custom_call_target="tpu_custom_call" | custom-call | tf_op jit(solution)/shard_map/pack/pallas_call | solution.py:45
  10.1 7.3 %all-to-all-start = ((bf16[16,51,16,128]{3,2,1,0:T(8,128)(2,1)}), bf16[16,51,16,128]{3,2,1,0:T(8,128)(2,1)S(1)}, u32[]{:S(2)}, u32[]{:S(2)}) async-start(bf16[16,51,16,128]{3,2,1,0:T(8,128)(2,1)} %pack.1), calls=%async_computation | async-start | bytes 6684672 | tf_op jit(solution)/shard_map/all_to_all | solution.py:372
  23.4 9.4 %basis.1.table_ref = bf16[4,640,1408]{2,1,0:T(8,128)(2,1)} custom-call(s32[1]{0:T(128)} %dynamic_slice.13.count_ref, s32[640,1]{1,0:T(8,128)S(1)} %copy-done.1), custom_call_target="tpu_custom_call" | custom-call | flops 200000000 | bytes 30000000 | tf_op jit(solution)/shard_map/basis/pallas_call | solution.py:229
  33.0 29.1 %all-to-all-done.main_ref.tail_ref = bf16[16,51,16,128]{3,2,1,0:T(8,128)(2,1)S(1)} async-done(((bf16[16,51,16,128]{3,2,1,0:T(8,128)(2,1)}), bf16[16,51,16,128]{3,2,1,0:T(8,128)(2,1)S(1)}, u32[]{:S(2)}, u32[]{:S(2)}) %all-to-all-start) | async-done | bytes 3342368 | tf_op jit(solution)/shard_map/all_to_all | solution.py:372
  62.1 7.4 %invert.1 = bf16[5,2,128,128]{3,2,1,0:T(8,128)(2,1)S(1)} custom-call(s32[5]{0:T(128)S(1)} %dynamic-slice_subtract_fusion.split_ref, bf16[16,51,16,128]{3,2,1,0:T(8,128)(2,1)S(1)} %all-to-all-done.main_ref.tail_ref, bf16[16,51,16,128]{3,2,1,0:T(8,128)(2,1)S(1)} %all-to-all-done.main_ref.tail_ref, bf16[256,128]{1,0:T(8,128)(2,1)S(1)} %fusion.pick_ref), custom_call_target="tpu_custom_call" | custom-call | tf_op jit(solution)/shard_map/invert/pallas_call | solution.py:87
  70.2 1.9 %copy.19 = bf16[128,2,5,128]{0,3,2,1:T(8,128)(2,1)} copy(bf16[128,2,5,128]{3,0,1,2:T(8,128)(2,1)} %bitcast.16) | data formatting | bytes 655360 | tf_op jit(solution)/shard_map/transpose | solution.py:390
  72.1 1.9 %copy.20 = bf16[128,2,640]{2,1,0:T(2,128)(2,1)} copy(bf16[128,2,640]{0,2,1:T(8,128)(2,1)} %bitcast.20) | data formatting | bytes 655360 | tf_op jit(solution)/shard_map/reshape | solution.py:390
  74.0 13.6 %all-to-all-start.1 = ((bf16[128,2,640]{2,1,0:T(2,128)(2,1)}), bf16[128,2,640]{2,1,0:T(2,128)(2,1)}, u32[]{:S(2)}, u32[]{:S(2)}) async-start(bf16[128,2,640]{2,1,0:T(2,128)(2,1)} %copy.20), calls=%async_computation.1 | async-start | bytes 655360 | tf_op jit(solution)/shard_map/all_to_all | solution.py:391
  87.7 11.2 %all-to-all-done.1 = bf16[128,2,640]{2,1,0:T(2,128)(2,1)} async-done(((bf16[128,2,640]{2,1,0:T(2,128)(2,1)}), bf16[128,2,640]{2,1,0:T(2,128)(2,1)}, u32[]{:S(2)}, u32[]{:S(2)}) %all-to-all-start.1) | async-done | bytes 327712 | tf_op jit(solution)/shard_map/all_to_all | solution.py:391
  98.9 1.9 %copy.21 = bf16[128,2,640]{0,2,1:T(8,128)(2,1)} copy(bf16[128,2,640]{2,1,0:T(2,128)(2,1)} %all-to-all-done.1) | data formatting | bytes 655360 | tf_op jit(solution)/shard_map/all_to_all | solution.py:391
  100.8 1.9 %copy.22 = bf16[2,5,128,128]{3,2,1,0:T(8,128)(2,1)} copy(bf16[2,5,128,128]{2,3,1,0:T(8,128)(2,1)} %bitcast.21) | data formatting | bytes 655360 | tf_op jit(solution)/shard_map/transpose | solution.py:392
  104.6 9.3 %grid.1 = (f32[64,5136]{1,0:T(8,128)S(1)}, bf16[2,640,128]{2,1,0:T(8,128)(2,1)S(1)}) custom-call(s32[1]{0:T(128)} %dynamic_slice.13.count_ref, f32[1]{0:T(128)} %dynamic_slice.14.weight_ref, s32[640,1]{1,0:T(8,128)S(1)} %copy-done.2, bf16[4,640,1408]{2,1,0:T(8,128)(2,1)} %basis.1.table_ref, bf16[128,128]{1,0:T(8,128)(2,1)S(1)} %fusion.2.eye_ref, ...), custom_call_target="tpu_custom_call" | custom-call | tf_op jit(solution)/shard_map/grid/pallas_call | solution.py:348
  115.7 1.9 %copy.24 = bf16[2,5,128,128]{2,3,1,0:T(8,128)(2,1)} copy(bf16[2,5,128,128]{3,2,1,0:T(8,128)(2,1)} %bitcast.19) | data formatting | bytes 655360 | tf_op jit(solution)/shard_map/reshape | solution.py:396
  117.6 1.9 %copy.25 = bf16[128,2,640]{2,1,0:T(2,128)(2,1)} copy(bf16[128,2,640]{0,2,1:T(8,128)(2,1)} %bitcast.22) | data formatting | bytes 655360 | tf_op jit(solution)/shard_map/reshape | solution.py:396
  119.5 5.7 %all-to-all-start.2 = ((bf16[128,2,640]{2,1,0:T(2,128)(2,1)}), bf16[128,2,640]{2,1,0:T(2,128)(2,1)}, u32[]{:S(2)}, u32[]{:S(2)}) async-start(bf16[128,2,640]{2,1,0:T(2,128)(2,1)} %copy.25), calls=%async_computation.2 | async-start | bytes 655360 | tf_op jit(solution)/shard_map/all_to_all | solution.py:397
  125.3 11.2 %all-to-all-done.2 = bf16[128,2,640]{2,1,0:T(2,128)(2,1)} async-done(((bf16[128,2,640]{2,1,0:T(2,128)(2,1)}), bf16[128,2,640]{2,1,0:T(2,128)(2,1)}, u32[]{:S(2)}, u32[]{:S(2)}) %all-to-all-start.2) | async-done | bytes 327712 | tf_op jit(solution)/shard_map/all_to_all | solution.py:397
  136.4 1.9 %copy.26 = bf16[128,2,640]{0,2,1:T(8,128)(2,1)} copy(bf16[128,2,640]{2,1,0:T(2,128)(2,1)} %all-to-all-done.2) | data formatting | bytes 655360 | tf_op jit(solution)/shard_map/all_to_all | solution.py:397
  138.4 1.9 %copy.27 = bf16[128,2,5,128]{3,0,1,2:T(8,128)(2,1)} copy(bf16[128,2,5,128]{0,3,2,1:T(8,128)(2,1)} %bitcast.23) | data formatting | bytes 655360 | tf_op jit(solution)/shard_map/reshape | solution.py:398
  141.2 5.6 %contract.1 = bf16[16,26,16,128]{3,2,1,0:T(8,128)(2,1)S(1)} custom-call(s32[5]{0:T(128)S(1)} %dynamic-slice_subtract_fusion.split_ref, bf16[16,51,16,128]{3,2,1,0:T(8,128)(2,1)S(1)} %all-to-all-done.main_ref.tail_ref, bf16[16,51,16,128]{3,2,1,0:T(8,128)(2,1)S(1)} %all-to-all-done.main_ref.tail_ref, bf16[128,128]{1,0:T(8,128)(2,1)S(1)} %fusion.3.order_ref, ...), custom_call_target="tpu_custom_call" | custom-call | tf_op jit(solution)/shard_map/contract/pallas_call | solution.py:136
  148.0 3.8 %all-to-all-start.3 = ((bf16[16,26,16,128]{3,2,1,0:T(8,128)(2,1)}), bf16[16,26,16,128]{3,2,1,0:T(8,128)(2,1)S(1)}, u32[]{:S(2)}, u32[]{:S(2)}) async-start(bf16[16,26,16,128]{3,2,1,0:T(8,128)(2,1)} %copy-done), calls=%async_computation.3 | async-start | bytes 3407872 | tf_op jit(solution)/shard_map/all_to_all | solution.py:401
  151.9 2.4 %copy.28 = f32[64,1,5136]{2,1,0:T(1,128)} copy(f32[64,1,5136]{2,0,1:T(8,128)S(1)} %bitcast.15) | data formatting | bytes 2629632
  154.3 22.6 %all-to-all-done.3.in_ref = bf16[16,26,16,128]{3,2,1,0:T(8,128)(2,1)S(1)} async-done(((bf16[16,26,16,128]{3,2,1,0:T(8,128)(2,1)}), bf16[16,26,16,128]{3,2,1,0:T(8,128)(2,1)S(1)}, u32[]{:S(2)}, u32[]{:S(2)}) %all-to-all-start.3) | async-done | bytes 1703968 | tf_op jit(solution)/shard_map/all_to_all | solution.py:401
  176.9 6.6 %unpack.1 = f32[4,80,2,1281]{3,2,1,0:T(2,128)} custom-call(bf16[16,26,16,128]{3,2,1,0:T(8,128)(2,1)S(1)} %all-to-all-done.3.in_ref), custom_call_target="tpu_custom_call" | custom-call | tf_op jit(solution)/shard_map/unpack/pallas_call | solution.py:171
  (43 shorter events, 12.5 us)
Async XLA Ops:
  0.6 1.5 copy-start.3
  2.1 1.5 copy-start.4
  10.1 7.3 %copy-start.12 = (s32[128]{0:T(128)S(1)}, s32[128]{0:T(128)}, u32[]{:S(2)}) copy-start(s32[128]{0:T(128)} %param.10) | copy-start | bytes 1540
  10.1 9.2 %copy-start.11 = (s32[640]{0:T(1024)S(1)}, s32[640]{0:T(1024)}, u32[]{:S(2)}) copy-start(s32[640]{0:T(1024)} %param.9) | copy-start | bytes 7684
  10.1 11.1 %copy-start.13 = (s32[128]{0:T(128)S(1)}, s32[128]{0:T(128)}, u32[]{:S(2)}) copy-start(s32[128]{0:T(128)} %param.11) | copy-start | bytes 1540
  10.1 11.8 %copy-start.14 = (f32[8]{0:T(128)S(1)}, f32[8]{0:T(128)}, u32[]{:S(2)}) copy-start(f32[8]{0:T(128)} %param.8) | copy-start | bytes 100
  10.1 52.0 %all-to-all-start = ((bf16[16,51,16,128]{3,2,1,0:T(8,128)(2,1)}), bf16[16,51,16,128]{3,2,1,0:T(8,128)(2,1)S(1)}, u32[]{:S(2)}, u32[]{:S(2)}) async-start(bf16[16,51,16,128]{3,2,1,0:T(8,128)(2,1)} %pack.1), calls=%async_computation | async-start | bytes 6684672 | tf_op jit(solution)/shard_map/all_to_all | solution.py:372
  22.5 1.0 copy-start.1
  69.5 0.7 copy-start.7
  74.0 24.9 %all-to-all-start.1 = ((bf16[128,2,640]{2,1,0:T(2,128)(2,1)}), bf16[128,2,640]{2,1,0:T(2,128)(2,1)}, u32[]{:S(2)}, u32[]{:S(2)}) async-start(bf16[128,2,640]{2,1,0:T(2,128)(2,1)} %copy.20), calls=%async_computation.1 | async-start | bytes 655360 | tf_op jit(solution)/shard_map/all_to_all | solution.py:391
  102.7 1.0 copy-start.2
  103.7 1.0 copy-start.8
  113.9 1.1 copy-start.5
  115.0 0.7 copy-start.10
  119.5 17.0 %all-to-all-start.2 = ((bf16[128,2,640]{2,1,0:T(2,128)(2,1)}), bf16[128,2,640]{2,1,0:T(2,128)(2,1)}, u32[]{:S(2)}, u32[]{:S(2)}) async-start(bf16[128,2,640]{2,1,0:T(2,128)(2,1)} %copy.25), calls=%async_computation.2 | async-start | bytes 655360 | tf_op jit(solution)/shard_map/all_to_all | solution.py:397
  140.2 1.0 copy-start.9
  146.8 1.2 copy-start
  148.0 3.9 %copy-start.6 = (f32[64,5136]{1,0:T(8,128)S(1)}, f32[64,5136]{1,0:T(8,128)}, u32[]{:S(2)}) copy-start(f32[64,5136]{1,0:T(8,128)} %copy-done.5) | copy-start | bytes 3944452
  148.0 28.9 %all-to-all-start.3 = ((bf16[16,26,16,128]{3,2,1,0:T(8,128)(2,1)}), bf16[16,26,16,128]{3,2,1,0:T(8,128)(2,1)S(1)}, u32[]{:S(2)}, u32[]{:S(2)}) async-start(bf16[16,26,16,128]{3,2,1,0:T(8,128)(2,1)} %copy-done), calls=%async_computation.3 | async-start | bytes 3407872 | tf_op jit(solution)/shard_map/all_to_all | solution.py:401

commit v2 on v1

v2 whole, which is shorter than its diff:
```python
import functools
import math

import jax
import jax.numpy as jnp
from jax import lax
from jax.experimental import pallas as pl
from jax.experimental.pallas import tpu as pltpu
from jax.sharding import PartitionSpec as P

TRUNC = 1279
COEFS = TRUNC + 2
LANES = 128
BLOCKS = (COEFS - 1) // LANES
QUARTER = 11
WIDTH = 4 * TRUNC + 20

f32 = jnp.float32
bf16 = jnp.bfloat16

NT = (((1,), (1,)), ((), ()))


def params(mib=32):
    return pltpu.CompilerParams(vmem_limit_bytes=mib * 1024 * 1024)


def pack_kernel(leg_ref, spec_ref, out_ref):
    dests = out_ref.shape[0]
    pairs = leg_ref.shape[0] // dests
    lane = lax.broadcasted_iota(jnp.int32, (16, LANES), 1)
    for d in range(dests):
        tail = jnp.zeros((16, LANES), f32)
        for p in range(pairs):
            at = d * pairs + p
            table = leg_ref[at].astype(f32)
            spec = jnp.concatenate([spec_ref[l, at].astype(f32) for l in range(4)], axis=0)
            rows = jnp.concatenate([table, spec], axis=0)
            for b in range(BLOCKS):
                out_ref[d, p * BLOCKS + b] = rows[:, b * LANES : (b + 1) * LANES].astype(bf16)
            tail = jnp.where(lane == p, rows[:, COEFS - 1 : COEFS], tail)
        out_ref[d, pairs * BLOCKS] = tail.astype(bf16)


def pack(legendre, spectral):
    pairs = legendre.shape[0] // 16
    dests = 4
    return pl.pallas_call(
        pack_kernel,
        grid=(16 // dests,),
        in_specs=[
            pl.BlockSpec((dests * pairs, 8, COEFS), lambda d: (d, 0, 0)),
            pl.BlockSpec((4, dests * pairs, 2, COEFS), lambda d: (0, d, 0, 0)),
        ],
        out_specs=pl.BlockSpec((dests, pairs * BLOCKS + 1, 16, LANES), lambda d: (d, 0, 0, 0)),
        out_shape=jax.ShapeDtypeStruct((16, pairs * BLOCKS + 1, 16, LANES), bf16),
        compiler_params=params(60),
        name="pack",
    )(legendre, spectral)


def halves(main_ref, tail_ref, which):
    parts = [main_ref[:, b] for b in range(BLOCKS)] + [tail_ref[:, 0]]
    first = which * 8
    return jnp.concatenate(
        [part.astype(f32)[:, first : first + 8].reshape(128, LANES).astype(bf16) for part in parts], axis=1
    )


def invert_kernel(split_ref, main_ref, tail_ref, pick_ref, out_ref, rows_ref):
    p = pl.program_id(0)
    split = split_ref[p]
    table = halves(main_ref, tail_ref, 0)
    data = halves(main_ref, tail_ref, 1)
    slot = lax.broadcasted_iota(jnp.int32, (16, data.shape[1]), 1)
    whole = BLOCKS * LANES
    first = (slot < split) & (slot < whole)
    second = ((slot >= split) & (slot < whole)) | (slot == whole + p)
    apart = data.reshape(8, 16, data.shape[1])
    for s, part in enumerate((first, second)):
        kept = (apart * jnp.where(part, 1.0, 0.0).astype(bf16)[None]).reshape(data.shape)
        sums = lax.dot_general(table, kept, NT, preferred_element_type=f32).astype(bf16)
        sums = jnp.dot(sums, pick_ref[...], preferred_element_type=f32)
        rows_ref[pl.ds(2 * p + s, 128, stride=2 * pl.num_programs(0)), :] = sums

    @pl.when(p == pl.num_programs(0) - 1)
    def _():
        out_ref[...] = rows_ref[...].astype(bf16)


def invert(splits, buffer, pick):
    pairs = splits.shape[0]
    rows = 2 * pairs * 128
    return pl.pallas_call(
        invert_kernel,
        grid=(pairs,),
        in_specs=[
            pl.BlockSpec(memory_space=pltpu.SMEM),
            pl.BlockSpec((16, BLOCKS, 16, LANES), lambda p: (0, p, 0, 0)),
            pl.BlockSpec((16, 1, 16, LANES), lambda p: (0, pairs * BLOCKS, 0, 0)),
            pl.BlockSpec((128, LANES), lambda p: (0, 0)),
        ],
        out_specs=pl.BlockSpec((rows, LANES), lambda p: (0, 0)),
        out_shape=jax.ShapeDtypeStruct((rows, LANES), bf16),
        scratch_shapes=[pltpu.VMEM((rows, LANES), f32)],
        compiler_params=params(),
        name="invert",
    )(splits, buffer, buffer, pick)


def contract_kernel(split_ref, main_ref, tail_ref, order_ref, back_ref, out_ref, rows_ref):
    p = pl.program_id(0)
    split = split_ref[p]

    @pl.when(p == 0)
    def _():
        rows_ref[...] = back_ref[...].astype(f32)

    data = halves(main_ref, tail_ref, 0)
    sums = []
    for s in range(2):
        back = rows_ref[pl.ds(2 * p + s, 128, stride=2 * pl.num_programs(0)), :].astype(bf16)
        turned = lax.dot_general(order_ref[...], back, NT, preferred_element_type=f32).astype(bf16)
        sums.append(jnp.dot(turned, data, preferred_element_type=f32))
    slot = lax.broadcasted_iota(jnp.int32, sums[0].shape, 1)
    result = jnp.where(slot < split, sums[0], sums[1])
    for b in range(0, BLOCKS, 2):
        left = result[:, b * LANES : (b + 1) * LANES].reshape(16, 8, LANES)
        right = result[:, (b + 1) * LANES : (b + 2) * LANES].reshape(16, 8, LANES)
        both = jnp.concatenate([left, right], axis=1).astype(bf16)
        out_ref[:, pl.ds(p * (BLOCKS // 2) + b // 2, 1)] = both[:, None]
    last = sums[1][:, BLOCKS * LANES :].reshape(16, 8, LANES)
    last = jnp.concatenate([last, last], axis=1)
    lane = lax.broadcasted_iota(jnp.int32, last.shape, 2)
    end = out_ref.shape[1] - 1

    @pl.when(p == 0)
    def _():
        out_ref[:, end] = jnp.where(lane == 0, last, 0.0).astype(bf16)

    @pl.when(p > 0)
    def _():
        out_ref[:, end] = jnp.where(lane == p, last, out_ref[:, end].astype(f32)).astype(bf16)


def contract(splits, buffer, order, back):
    pairs = splits.shape[0]
    out_blocks = pairs * BLOCKS // 2 + 1
    rows = 2 * pairs * 128
    return pl.pallas_call(
        contract_kernel,
        grid=(pairs,),
        in_specs=[
            pl.BlockSpec(memory_space=pltpu.SMEM),
            pl.BlockSpec((16, BLOCKS, 16, LANES), lambda p: (0, p, 0, 0)),
            pl.BlockSpec((16, 1, 16, LANES), lambda p: (0, pairs * BLOCKS, 0, 0)),
            pl.BlockSpec((128, LANES), lambda p: (0, 0)),
            pl.BlockSpec((rows, LANES), lambda p: (0, 0)),
        ],
        out_specs=pl.BlockSpec((16, out_blocks, 16, LANES), lambda p: (0, 0, 0, 0)),
        out_shape=jax.ShapeDtypeStruct((16, out_blocks, 16, LANES), bf16),
        scratch_shapes=[pltpu.VMEM((rows, LANES), f32)],
        compiler_params=params(),
        name="contract",
    )(splits, buffer, buffer, order, back)


def unpack_kernel(in_ref, out_ref, rows_ref):
    senders = in_ref.shape[0]
    pairs = out_ref.shape[1] // senders
    blocks = in_ref.shape[1]
    for d in range(senders):
        rows_ref[...] = in_ref[d].astype(f32)
        for p in range(pairs):
            for b in range(BLOCKS):
                for l in range(4):
                    pair = rows_ref[p * (BLOCKS // 2) + b // 2, pl.ds(b % 2 * 8 + 2 * l, 2), :]
                    out_ref[l, d * pairs + p, :, b * LANES : (b + 1) * LANES] = pair
            for l in range(4):
                last = rows_ref[blocks - 1, pl.ds(2 * l, 2), :]
                out_ref[l, d * pairs + p, :, COEFS - 1 : COEFS] = last[:, p : p + 1]


def unpack(buffer, pairs):
    blocks = buffer.shape[1]
    senders = 4
    return pl.pallas_call(
        unpack_kernel,
        grid=(16 // senders,),
        in_specs=[pl.BlockSpec((senders, blocks, 16, LANES), lambda d: (d, 0, 0, 0))],
        out_specs=pl.BlockSpec((4, senders * pairs, 2, COEFS), lambda d: (0, d, 0, 0)),
        out_shape=jax.ShapeDtypeStruct((4, 16 * pairs, 2, COEFS), f32),
        scratch_shapes=[pltpu.VMEM((blocks, 16, LANES), f32)],
        compiler_params=params(),
        name="unpack",
    )(buffer)


def turn(whole, part):
    scaled = part * (4.0 / whole)
    nearest = jnp.floor(scaled + 0.5)
    angle = (scaled - nearest) * (math.pi / 2)
    square = angle * angle
    sine = angle + angle * square * (
        -1.6666654611e-1 + square * (8.3321608736e-3 - 1.9515295891e-4 * square)
    )
    cosine = 1.0 - 0.5 * square + square * square * (
        4.166664568298827e-2 + square * (-1.388731625493765e-3 + 2.443315711809948e-5 * square)
    )
    odd = (nearest == 1.0) | (nearest == 3.0)
    cos_base = jnp.where(odd, sine, cosine)
    sin_base = jnp.where(odd, cosine, sine)
    cos_sign = jnp.where((nearest == 1.0) | (nearest == 2.0), -1.0, 1.0)
    sin_sign = jnp.where((nearest == 2.0) | (nearest == 3.0), -1.0, 1.0)
    return cos_base * cos_sign, sin_base * sin_sign


def remainder(value, whole):
    quotient = jnp.floor(value * (1.0 / whole))
    rest = value - quotient * whole
    rest = jnp.where(rest < 0.0, rest + whole, rest)
    return jnp.where(rest >= whole, rest - whole, rest)


def upright_column(row):
    return jnp.broadcast_to(row.astype(f32), (LANES, LANES)).T


def basis_kernel(count_ref, order_ref, out_ref):
    whole = count_ref[0].astype(f32)
    order = upright_column(order_ref[pl.ds(pl.program_id(0), 1), :])
    rows = LANES
    even = jnp.where(remainder(order, 2.0) < 0.5, order, TRUNC - order)
    lane = lax.broadcasted_iota(jnp.int32, (rows, LANES), 1).astype(f32)
    for kind in range(2):
        wave = even if kind == 0 else TRUNC - even
        cos_fine, sin_fine = turn(whole, remainder(wave * lane, whole))
        cos_coarse, sin_coarse = turn(whole, remainder(wave * (lane * 128.0), whole))
        for a in range(QUARTER):
            cos_a = cos_coarse[:, a : a + 1]
            sin_a = sin_coarse[:, a : a + 1]
            at = pl.ds(a * LANES, LANES)
            out_ref[2 * kind, :, at] = (cos_a * cos_fine - sin_a * sin_fine).astype(bf16)
            out_ref[2 * kind + 1, :, at] = (sin_a * cos_fine + cos_a * sin_fine).astype(bf16)


def basis(count, order):
    rows = LANES
    pairs = order.size
    return pl.pallas_call(
        basis_kernel,
        grid=(pairs // rows,),
        in_specs=[
            pl.BlockSpec(memory_space=pltpu.SMEM),
            pl.BlockSpec(order.shape, lambda i: (0, 0)),
        ],
        out_specs=pl.BlockSpec((4, rows, QUARTER * LANES), lambda i: (0, i, 0)),
        out_shape=jax.ShapeDtypeStruct((4, pairs, QUARTER * LANES), bf16),
        compiler_params=params(),
        cost_estimate=pl.CostEstimate(flops=200_000_000, bytes_accessed=30_000_000, transcendentals=0),
        name="basis",
    )(count, order)


def grid_kernel(count_ref, weight_ref, order_ref, table_ref, eye_ref, in_ref, grid_ref, back_ref, place, rows_ref):
    count = count_ref[0]
    quarter = count // 4
    length = count.astype(f32)
    whole = jnp.full((1, LANES), length)
    shrink = lax.rsqrt(whole)
    groups = order_ref.shape[0]
    pairs = groups * LANES
    order = jnp.concatenate([upright_column(order_ref[pl.ds(i, 1), :]) for i in range(groups)], axis=0)
    swap = remainder(order, 2.0) < 0.5
    even = jnp.where(swap, order, TRUNC - order)
    odd = TRUNC - even
    left = lax.broadcasted_iota(jnp.int32, (pairs, LANES), 1) < 64
    sign_even = jnp.where(remainder(even, 4.0) < 0.5, 1.0, -1.0)
    sign_odd = jnp.where(remainder(odd, 4.0) < 1.5, 1.0, -1.0)
    keep_even = jnp.where(2.0 * even < length, jnp.where(even < 0.5, 1.0, 2.0), 0.0)
    keep_odd = jnp.where(2.0 * odd < length, 2.0, 0.0)
    rows_ref[...] = in_ref[...].astype(f32)

    def arrived(s):
        parts = [rows_ref[pl.ds(2 * i + s, LANES, stride=2 * groups), :] for i in range(groups)]
        return jnp.concatenate(parts, axis=0)

    first = arrived(0)
    second = arrived(1)
    coef_even = jnp.where(swap, first, second) * keep_even
    coef_odd = jnp.where(swap, second, first) * keep_odd
    turned_even = pltpu.roll(coef_even, 64, 1)
    turned_odd = pltpu.roll(coef_odd, 64, 1)
    even_cos = jnp.where(left, coef_even, turned_even * sign_even)
    even_sin = -jnp.where(left, turned_even, coef_even * sign_even)
    odd_cos = jnp.where(left, coef_odd, -(coef_odd * sign_odd))
    odd_sin = -jnp.where(left, turned_odd, turned_odd * sign_odd)

    def upright(values):
        return lax.dot_general(eye_ref[...], values.astype(bf16), NT, preferred_element_type=f32).astype(bf16)

    sum_even = jnp.dot(upright(even_cos), table_ref[0], preferred_element_type=f32)
    sum_even += jnp.dot(upright(even_sin), table_ref[1], preferred_element_type=f32)
    sum_odd = jnp.dot(upright(odd_cos), table_ref[2], preferred_element_type=f32)
    sum_odd += jnp.dot(upright(odd_sin), table_ref[3], preferred_element_type=f32)

    width = QUARTER * LANES
    along = lax.broadcasted_iota(jnp.int32, (1, width), 1)
    factor = jnp.where(along < quarter, jnp.broadcast_to(shrink[:, :1], (1, width)), 0.0)
    near = (sum_even + sum_odd) * factor
    far = (sum_even - sum_odd) * factor

    place[...] = jnp.zeros_like(place)
    narrow = lax.broadcasted_iota(jnp.int32, (64, LANES), 1)
    for t, field in enumerate((near[:64], near[64:], far[:64], far[64:])):
        start = t * quarter
        shift = start % LANES
        base = start // LANES
        before = jnp.zeros((64, LANES), f32)
        for b in range(QUARTER + 1):
            if b < QUARTER:
                block = field[:, b * LANES : (b + 1) * LANES]
                block = pltpu.roll(block, shift, 1)
            else:
                block = jnp.zeros((64, LANES), f32)
            merged = jnp.where(narrow < shift, before, block)
            at = pl.ds(pl.multiple_of((base + b) * LANES, LANES), LANES)
            place[:, at] += merged
            before = block
    grid_ref[...] = place[:, :WIDTH]

    def product(field):
        return jnp.concatenate(
            [
                half * jnp.concatenate([half[1:], half[:1]], axis=0)
                for half in (field[:64], field[64:])
            ],
            axis=0,
        )

    near = product(near)
    far = product(far)
    both = (near + far).astype(bf16)
    gap = (near - far).astype(bf16)

    def analyse(index, values):
        return lax.dot_general(table_ref[index], values, NT, preferred_element_type=f32)

    x_cos = analyse(0, both)
    x_sin = analyse(1, both)
    y_cos = analyse(2, gap)
    y_sin = analyse(3, gap)
    scale = weight_ref[0] * shrink
    back_even = jnp.where(
        left,
        x_cos + sign_even * pltpu.roll(x_cos, 64, 1),
        -(sign_even * x_sin + pltpu.roll(x_sin, 64, 1)),
    )
    turned = pltpu.roll(y_sin, 64, 1)
    back_odd = jnp.where(left, y_cos - sign_odd * turned, -turned - sign_odd * y_cos)
    back_even = jnp.where(keep_even > 0.0, back_even * scale, 0.0)
    back_odd = jnp.where(keep_odd > 0.0, back_odd * scale, 0.0)
    leaving = (jnp.where(swap, back_even, back_odd), jnp.where(swap, back_odd, back_even))
    for s in range(2):
        for i in range(groups):
            part = leaving[s][i * LANES : (i + 1) * LANES]
            rows_ref[pl.ds(2 * i + s, LANES, stride=2 * groups), :] = part
    back_ref[...] = rows_ref[...].astype(bf16)


def grid_step(count, weight, order, table, eye, coeffs):
    rows = 2 * order.size
    smem = pl.BlockSpec(memory_space=pltpu.SMEM)
    vmem = pl.BlockSpec(memory_space=pltpu.VMEM)
    return pl.pallas_call(
        grid_kernel,
        in_specs=[smem, smem, vmem, vmem, vmem, vmem],
        out_specs=[vmem, vmem],
        out_shape=[
            jax.ShapeDtypeStruct((64, WIDTH), f32),
            jax.ShapeDtypeStruct((rows, LANES), bf16),
        ],
        scratch_shapes=[
            pltpu.VMEM((64, (4 * QUARTER + 2) * LANES), f32),
            pltpu.VMEM((rows, LANES), f32),
        ],
        compiler_params=params(),
        name="grid",
    )(count, weight, order, table, eye, coeffs)


def shards(spectral_in, legendre, weights, pair_order, row_lat, lon_count):
    band_count = lax.axis_size("band")
    lev_count = lax.axis_size("lev")
    band_place = lax.axis_index("band")
    lev_place = lax.axis_index("lev")
    devices = band_count * lev_count
    pairs_dev = legendre.shape[0]
    pairs = pairs_dev // lev_count
    all_pairs = pair_order.shape[0]

    buffer = lax.all_to_all(pack(legendre, spectral_in), "lev", 0, 0, tiled=True)

    my_row = lax.dynamic_slice_in_dim(row_lat, lev_place * band_count + band_place, 1)
    my_count = lax.dynamic_slice_in_dim(lon_count, my_row[0], 1)
    my_weight = lax.dynamic_slice_in_dim(weights, band_place, 1)
    my_orders = lax.dynamic_slice_in_dim(pair_order, band_place * pairs_dev + lev_place * pairs, pairs)
    splits = TRUNC + 1 - my_orders
    arrived = pair_order.reshape(band_count, lev_count, pairs).transpose(2, 1, 0).reshape(pairs, devices)
    table = basis(my_count, arrived)

    lane = jnp.arange(LANES, dtype=jnp.int32)
    pick = (lane[:, None] == (2 * (lane % 64) + lane // 64)[None, :]).astype(bf16)
    eye = (lane[:, None] == lane[None, :]).astype(bf16)

    def exchange(rows):
        rows = rows.reshape(devices, pairs, 2, LANES)
        return lax.all_to_all(rows, ("lev", "band"), 0, 0, tiled=True).reshape(2 * all_pairs, LANES)

    fourier = exchange(invert(splits, buffer, pick))
    grid_row, back = grid_step(my_count, my_weight, arrived, table, eye, fourier)
    spectral = contract(splits, buffer, pick, exchange(back))
    spectral = lax.all_to_all(spectral, "lev", 0, 0, tiled=True)
    return (grid_row.reshape(64, 1, WIDTH), unpack(spectral, pairs))


def solution(mesh):
    return jax.shard_map(
        shards,
        mesh=mesh,
        in_specs=(P("lev", "band", None, None), P("band", "lev", None), P("lev"), P(), P(), P()),
        out_specs=(P(None, ("lev", "band"), None), P("lev", "band", None, None)),
        check_vma=False,
    )
```

time: 184 us -> 161 us (0.88)
  blocking collectives: 0 us -> 21.1 us
  local copies, waits for them, and re-layouts: 31.3 us -> 13.6 us
  Pallas kernels: 44.8 us -> 31.4 us
  waiting for transfers between devices: 74.1 us -> 67.2 us
  starting transfers between devices: 30.4 us -> 24.7 us
    all_to_all x2 -> x1, waiting for transfers between devices: 22.4 us -> 0.01 us  [exchange(): lax.all_to_all(rows, ('lev', 'band'), 0, 0, tiled=True)]
    all_to_all x0 -> x1, blocking collectives: none -> 21.1 us  [exchange(): lax.all_to_all(rows, ('lev', 'band'), 0, 0, tiled=True)]
    all_to_all x1, waiting for transfers between devices: 29.1 us -> 44.6 us  [shards(): lax.all_to_all(pack(legendre, spectral_in), 'lev', 0, 0, tiled=True)]
    reshape x4 -> x0, local copies, waits for them, and re-layouts: 7.55 us -> none  [the longest x2 3.78 us: shards(): back.reshape(2, pairs, devices, LANES).transpose(2, 0, 1, 3)]
    all_to_all x2 -> x1, starting transfers between devices: 19.3 us -> 13.6 us  [exchange(): lax.all_to_all(rows, ('lev', 'band'), 0, 0, tiled=True)]
    pallas_call x2, Pallas kernels: 13.1 us -> 7.97 us  [the longest x1 4.88 us: pack(): pl.pallas_call(pack_kernel, grid=(16 // dests,), in_specs=[pl.BlockSpec((...]
    all_to_all x2 -> x0, local copies, waits for them, and re-layouts: 3.81 us -> none  [the longest x1 1.91 us: shards(): fourier = lax.all_to_all(fourier, ('lev', 'band'), 0, 0, tiled=True)]
    transpose x2 -> x0, local copies, waits for them, and re-layouts: 3.73 us -> none  [the longest x1 1.86 us: shards(): jnp.transpose(fourier, (2, 1, 0, 3)).reshape(devices, 2, pairs * LANES)]
  transfers between devices with their start and end apart: 4 -> 3, of which waited for: 4 -> 2; matrix products, arithmetic and copies ran while one was open for 3% -> 3% of each run, Pallas kernels for 5% -> 4%
where the time goes in v2:
time: 161 us
  waiting for transfers between devices  67.2 us (42%)
  Pallas kernels  31.4 us (20%)
  starting transfers between devices  24.7 us (15%)
  blocking collectives  21.1 us (13%)
  local copies, waits for them, and re-layouts  13.6 us (8%)
  between operations  2.79 us (2%)
    all_to_all x1, waiting for transfers between devices, shards(): lax.all_to_all(pack(legendre, spectral_in), 'lev', 0, 0, tiled=True)  44.6 us
    all_to_all x1, waiting for transfers between devices, shards(): spectral = lax.all_to_all(spectral, 'lev', 0, 0, tiled=True)  22.6 us
    all_to_all x1, blocking collectives, exchange(): lax.all_to_all(rows, ('lev', 'band'), 0, 0, tiled=True)  21.1 us
    all_to_all x1, starting transfers between devices, exchange(): lax.all_to_all(rows, ('lev', 'band'), 0, 0, tiled=True)  13.6 us
    unnamed x21, local copies, waits for them, and re-layouts  11.4 us
    all_to_all x1, starting transfers between devices, shards(): lax.all_to_all(pack(legendre, spectral_in), 'lev', 0, 0, tiled=True)  7.25 us
    pallas_call x1, Pallas kernels, basis(): pl.pallas_call(basis_kernel, grid=(pairs // rows,), in_specs=[pl.BlockSpe...  7.18 us
    pallas_call x1, Pallas kernels, grid_step(): pl.pallas_call(grid_kernel, in_specs=[smem, smem, vmem, vmem, vmem, vmem]...  7 us
  transfers between devices with their start and end apart: 3, of which 2 were waited for; matrix products, arithmetic and copies ran while one was open for 3% of the time, Pallas kernels for 4%

profile of v2, /device:TPU:0, one launch (start us, length us, event | category | flops | bytes accessed | tf_op | source)
XLA Modules:
  0.0 160.9 jit_solution(2271418354199197179)
XLA Ops:
  0.6 4.9 %pack.1 = bf16[16,51,16,128]{3,2,1,0:T(8,128)(2,1)} custom-call(bf16[80,8,1281]{2,1,0:T(8,128)(2,1)} %leg_ref.1, bf16[4,80,2,1281]{3,2,1,0:T(2,128)(2,1)} %spec_ref.1), custom_call_target="tpu_custom_call" | custom-call | tf_op jit(solution)/shard_map/pack/pallas_call | solution.py:48
  5.5 7.2 %all-to-all-start = ((bf16[16,51,16,128]{3,2,1,0:T(8,128)(2,1)}), bf16[16,51,16,128]{3,2,1,0:T(8,128)(2,1)S(1)}, u32[]{:S(2)}, u32[]{:S(2)}) async-start(bf16[16,51,16,128]{3,2,1,0:T(8,128)(2,1)} %pack.1), calls=%async_computation | async-start | bytes 6684672 | tf_op jit(solution)/shard_map/all_to_all | solution.py:402
  12.9 44.6 %all-to-all-done.main_ref.tail_ref = bf16[16,51,16,128]{3,2,1,0:T(8,128)(2,1)S(1)} async-done(((bf16[16,51,16,128]{3,2,1,0:T(8,128)(2,1)}), bf16[16,51,16,128]{3,2,1,0:T(8,128)(2,1)S(1)}, u32[]{:S(2)}, u32[]{:S(2)}) %all-to-all-start) | async-done | bytes 3342368 | tf_op jit(solution)/shard_map/all_to_all | solution.py:402
  57.5 4.9 %invert.1 = bf16[1280,128]{1,0:T(8,128)(2,1)S(1)} custom-call(s32[5]{0:T(128)S(1)} %dynamic-slice_subtract_fusion.split_ref, bf16[16,51,16,128]{3,2,1,0:T(8,128)(2,1)S(1)} %all-to-all-done.main_ref.tail_ref, bf16[16,51,16,128]{3,2,1,0:T(8,128)(2,1)S(1)} %all-to-all-done.main_ref.tail_ref, bf16[128,128]{1,0:T(8,128)(2,1)S(1)} %fusion.1.pick_ref.order_ref), custom_call_target="tpu_custom_call" | custom-call | tf_op jit(solution)/shard_map/invert/pallas_call | solution.py:94
  62.4 0.7 copy-done.5
  63.1 13.6 %all-to-all-start.1 = ((bf16[128,5,2,128]{3,2,1,0:T(2,128)(2,1)}), bf16[128,5,2,128]{3,2,1,0:T(2,128)(2,1)}, u32[]{:S(2)}, u32[]{:S(2)}) async-start(bf16[128,5,2,128]{3,2,1,0:T(2,128)(2,1)} %bitcast.8), calls=%async_computation.1 | async-start | bytes 655360 | tf_op jit(solution)/shard_map/all_to_all | solution.py:418
  76.8 0.6 dynamic_slice.12
  78.7 0.2 reshape.47
  78.9 0.2 copy.9
  79.0 0.1 reshape.48.order_ref
  79.8 0.6 dynamic_slice.13.count_ref
  80.4 0.6 dynamic_slice.14.weight_ref
  81.0 7.2 %basis.1.table_ref = bf16[4,640,1408]{2,1,0:T(8,128)(2,1)S(1)} custom-call(s32[1]{0:T(128)} %dynamic_slice.13.count_ref, s32[5,128]{1,0:T(8,128)S(1)} %reshape.48.order_ref), custom_call_target="tpu_custom_call" | custom-call | flops 200000000 | bytes 30000000 | tf_op jit(solution)/shard_map/basis/pallas_call | solution.py:250
  88.2 2.9 %copy-done = bf16[4,640,1408]{2,1,0:T(8,128)(2,1)} copy-done((bf16[4,640,1408]{2,1,0:T(8,128)(2,1)}, bf16[4,640,1408]{2,1,0:T(8,128)(2,1)S(1)}, u32[]{:S(2)}) %copy-start) | copy-done | bytes 7208984
  91.1 3.0 %copy-done.1 = bf16[4,640,1408]{2,1,0:T(8,128)(2,1)S(1)} copy-done((bf16[4,640,1408]{2,1,0:T(8,128)(2,1)S(1)}, bf16[4,640,1408]{2,1,0:T(8,128)(2,1)}, u32[]{:S(2)}) %copy-start.1) | copy-done | bytes 7208984
  94.1 7.0 %grid.1 = (f32[64,5136]{1,0:T(8,128)S(1)}, bf16[1280,128]{1,0:T(8,128)(2,1)S(1)}) custom-call(s32[1]{0:T(128)} %dynamic_slice.13.count_ref, f32[1]{0:T(128)} %dynamic_slice.14.weight_ref, s32[5,128]{1,0:T(8,128)S(1)} %reshape.48.order_ref, bf16[4,640,1408]{2,1,0:T(8,128)(2,1)S(1)} %copy-done.1, bf16[128,128]{1,0:T(8,128)(2,1)S(1)} %fusion.eye_ref, ...), custom_call_target="tpu_custom_call" | custom-call | tf_op jit(solution)/shard_map/grid/pallas_call | solution.py:375
  101.2 1.1 copy-done.3
  102.2 21.1 %all_to_all.20 = bf16[128,5,2,128]{3,2,1,0:T(2,128)(2,1)S(1)} all-to-all(bf16[128,5,2,128]{3,2,1,0:T(2,128)(2,1)S(1)} %bitcast.10), channel_id=1, replica_groups=mesh['band'=8,'lev'=16] {'lev','band'}, dimensions={0} | all-to-all | bytes 655360 | tf_op jit(solution)/shard_map/all_to_all | solution.py:418
  123.4 4.4 %contract.1 = bf16[16,26,16,128]{3,2,1,0:T(8,128)(2,1)S(1)} custom-call(s32[5]{0:T(128)S(1)} %dynamic-slice_subtract_fusion.split_ref, bf16[16,51,16,128]{3,2,1,0:T(8,128)(2,1)S(1)} %all-to-all-done.main_ref.tail_ref, bf16[16,51,16,128]{3,2,1,0:T(8,128)(2,1)S(1)} %all-to-all-done.main_ref.tail_ref, bf16[128,128]{1,0:T(8,128)(2,1)S(1)} %fusion.1.pick_ref.order_ref, ...), custom_call_target="tpu_custom_call" | custom-call | tf_op jit(solution)/shard_map/contract/pallas_call | solution.py:150
  127.7 1.2 copy-done.2
  128.9 3.8 %all-to-all-start.3 = ((bf16[16,26,16,128]{3,2,1,0:T(8,128)(2,1)}), bf16[16,26,16,128]{3,2,1,0:T(8,128)(2,1)S(1)}, u32[]{:S(2)}, u32[]{:S(2)}) async-start(bf16[16,26,16,128]{3,2,1,0:T(8,128)(2,1)} %copy-done.2), calls=%async_computation.3 | async-start | bytes 3407872 | tf_op jit(solution)/shard_map/all_to_all | solution.py:423
  132.8 2.4 %copy.10 = f32[64,1,5136]{2,1,0:T(1,128)} copy(f32[64,1,5136]{2,0,1:T(8,128)S(1)} %bitcast.7) | data formatting | bytes 2629632
  135.2 22.6 %all-to-all-done.3.in_ref = bf16[16,26,16,128]{3,2,1,0:T(8,128)(2,1)S(1)} async-done(((bf16[16,26,16,128]{3,2,1,0:T(8,128)(2,1)}), bf16[16,26,16,128]{3,2,1,0:T(8,128)(2,1)S(1)}, u32[]{:S(2)}, u32[]{:S(2)}) %all-to-all-start.3) | async-done | bytes 1703968 | tf_op jit(solution)/shard_map/all_to_all | solution.py:423
  157.8 3.1 %unpack.1 = f32[4,80,2,1281]{3,2,1,0:T(2,128)} custom-call(bf16[16,26,16,128]{3,2,1,0:T(8,128)(2,1)S(1)} %all-to-all-done.3.in_ref), custom_call_target="tpu_custom_call" | custom-call | tf_op jit(solution)/shard_map/unpack/pallas_call | solution.py:187
  (20 shorter events, 0.2 us)
Async XLA Ops:
  5.5 7.3 %copy-start.6 = (s32[640]{0:T(1024)S(1)}, s32[640]{0:T(1024)}, u32[]{:S(2)}) copy-start(s32[640]{0:T(1024)} %param.9) | copy-start | bytes 7684
  5.5 52.0 %all-to-all-start = ((bf16[16,51,16,128]{3,2,1,0:T(8,128)(2,1)}), bf16[16,51,16,128]{3,2,1,0:T(8,128)(2,1)S(1)}, u32[]{:S(2)}, u32[]{:S(2)}) async-start(bf16[16,51,16,128]{3,2,1,0:T(8,128)(2,1)} %pack.1), calls=%async_computation | async-start | bytes 6684672 | tf_op jit(solution)/shard_map/all_to_all | solution.py:402
  12.9 63.9 %copy-start.7 = (s32[128]{0:T(128)S(1)}, s32[128]{0:T(128)}, u32[]{:S(2)}) copy-start(s32[128]{0:T(128)} %param.10) | copy-start | bytes 1540
  12.9 66.9 %copy-start.8 = (s32[128]{0:T(128)S(1)}, s32[128]{0:T(128)}, u32[]{:S(2)}) copy-start(s32[128]{0:T(128)} %param.11) | copy-start | bytes 1540
  12.9 67.5 %copy-start.9 = (f32[8]{0:T(128)S(1)}, f32[8]{0:T(128)}, u32[]{:S(2)}) copy-start(f32[8]{0:T(128)} %param.8) | copy-start | bytes 100
  62.4 0.7 copy-start.5
  63.1 28.0 %all-to-all-start.1 = ((bf16[128,5,2,128]{3,2,1,0:T(2,128)(2,1)}), bf16[128,5,2,128]{3,2,1,0:T(2,128)(2,1)}, u32[]{:S(2)}, u32[]{:S(2)}) async-start(bf16[128,5,2,128]{3,2,1,0:T(2,128)(2,1)} %bitcast.8), calls=%async_computation.1 | async-start | bytes 655360 | tf_op jit(solution)/shard_map/all_to_all | solution.py:418
  88.2 2.9 %copy-start = (bf16[4,640,1408]{2,1,0:T(8,128)(2,1)}, bf16[4,640,1408]{2,1,0:T(8,128)(2,1)S(1)}, u32[]{:S(2)}) copy-start(bf16[4,640,1408]{2,1,0:T(8,128)(2,1)S(1)} %basis.1.table_ref) | copy-start | bytes 21626884
  91.1 3.0 %copy-start.1 = (bf16[4,640,1408]{2,1,0:T(8,128)(2,1)S(1)}, bf16[4,640,1408]{2,1,0:T(8,128)(2,1)}, u32[]{:S(2)}) copy-start(bf16[4,640,1408]{2,1,0:T(8,128)(2,1)} %copy-done) | copy-start | bytes 21626884
  101.2 1.1 copy-start.3
  127.7 1.2 copy-start.2
  128.9 3.9 %copy-start.4 = (f32[64,5136]{1,0:T(8,128)S(1)}, f32[64,5136]{1,0:T(8,128)}, u32[]{:S(2)}) copy-start(f32[64,5136]{1,0:T(8,128)} %copy-done.3) | copy-start | bytes 3944452
  128.9 28.9 %all-to-all-start.3 = ((bf16[16,26,16,128]{3,2,1,0:T(8,128)(2,1)}), bf16[16,26,16,128]{3,2,1,0:T(8,128)(2,1)S(1)}, u32[]{:S(2)}, u32[]{:S(2)}) async-start(bf16[16,26,16,128]{3,2,1,0:T(8,128)(2,1)} %copy-done.2), calls=%async_computation.3 | async-start | bytes 3407872 | tf_op jit(solution)/shard_map/all_to_all | solution.py:423

commit v3 on v2

--- a/solution.py
+++ b/solution.py
@@ -22,14 +22,51 @@
 
 
 def params(mib=32):
-    return pltpu.CompilerParams(vmem_limit_bytes=mib * 1024 * 1024)
-
-
-def pack_kernel(leg_ref, spec_ref, out_ref):
+    return pltpu.CompilerParams(vmem_limit_bytes=int(mib * 1024 * 1024))
+
+
+def own_place():
+    return lax.axis_index("band"), lax.axis_index("lev")
+
+
+def own_split(order_ref, pairs):
+    band, lev = own_place()
+    return TRUNC + 1 - order_ref[(band * lax.axis_size("lev") + lev) * pairs + pl.program_id(0)]
+
+
+def own_count(row_lat_ref, lon_count_ref):
+    band, lev = own_place()
+    return lon_count_ref[row_lat_ref[lev * lax.axis_size("band") + band]]
+
+
+def pick_matrix():
+    row = lax.broadcasted_iota(jnp.int32, (LANES, LANES), 0)
+    lane = lax.broadcasted_iota(jnp.int32, (LANES, LANES), 1)
+    return jnp.where(row == 2 * (lane % 64) + lane // 64, 1.0, 0.0).astype(bf16)
+
+
+def pack_kernel(leg_hbm, spec_hbm, out_ref, leg_ref, spec_ref, sems):
     dests = out_ref.shape[0]
     pairs = leg_ref.shape[0] // dests
+    steps = sems.shape[0]
+    size = leg_ref.shape[0] // steps
+    copies = []
+    for i in range(steps):
+        part = pl.ds(i * size, size)
+        copies.append(
+            (
+                pltpu.make_async_copy(leg_hbm.at[part], leg_ref.at[part], sems.at[i, 0]),
+                pltpu.make_async_copy(spec_hbm.at[:, part], spec_ref.at[:, part], sems.at[i, 1]),
+            )
+        )
+    for pair in copies:
+        for copy in pair:
+            copy.start()
     lane = lax.broadcasted_iota(jnp.int32, (16, LANES), 1)
     for d in range(dests):
+        if d % (dests // steps) == 0:
+            for copy in copies[d // (dests // steps)]:
+                copy.wait()
         tail = jnp.zeros((16, LANES), f32)
         for p in range(pairs):
             at = d * pairs + p
@@ -44,16 +81,17 @@
 
 def pack(legendre, spectral):
     pairs = legendre.shape[0] // 16
-    dests = 4
+    hbm = pl.BlockSpec(memory_space=pltpu.HBM)
     return pl.pallas_call(
         pack_kernel,
-        grid=(16 // dests,),
-        in_specs=[
-            pl.BlockSpec((dests * pairs, 8, COEFS), lambda d: (d, 0, 0)),
-            pl.BlockSpec((4, dests * pairs, 2, COEFS), lambda d: (0, d, 0, 0)),
-        ],
-        out_specs=pl.BlockSpec((dests, pairs * BLOCKS + 1, 16, LANES), lambda d: (d, 0, 0, 0)),
+        in_specs=[hbm, hbm],
+        out_specs=pl.BlockSpec(memory_space=pltpu.VMEM),
         out_shape=jax.ShapeDtypeStruct((16, pairs * BLOCKS + 1, 16, LANES), bf16),
+        scratch_shapes=[
+            pltpu.VMEM(legendre.shape, bf16),
+            pltpu.VMEM(spectral.shape, bf16),
+            pltpu.SemaphoreType.DMA((8, 2)),
+        ],
         compiler_params=params(60),
         name="pack",
     )(legendre, spectral)
@@ -67,9 +105,10 @@
     )
 
 
-def invert_kernel(split_ref, main_ref, tail_ref, pick_ref, out_ref, rows_ref):
+def invert_kernel(order_ref, main_ref, tail_ref, out_ref, rows_ref):
     p = pl.program_id(0)
-    split = split_ref[p]
+    split = own_split(order_ref, pl.num_programs(0))
+    pick = pick_matrix()
     table = halves(main_ref, tail_ref, 0)
     data = halves(main_ref, tail_ref, 1)
     slot = lax.broadcasted_iota(jnp.int32, (16, data.shape[1]), 1)
@@ -80,7 +119,7 @@
     for s, part in enumerate((first, second)):
         kept = (apart * jnp.where(part, 1.0, 0.0).astype(bf16)[None]).reshape(data.shape)
         sums = lax.dot_general(table, kept, NT, preferred_element_type=f32).astype(bf16)
-        sums = jnp.dot(sums, pick_ref[...], preferred_element_type=f32)
+        sums = jnp.dot(sums, pick, preferred_element_type=f32)
         rows_ref[pl.ds(2 * p + s, 128, stride=2 * pl.num_programs(0)), :] = sums
 
     @pl.when(p == pl.num_programs(0) - 1)
@@ -88,8 +127,8 @@
         out_ref[...] = rows_ref[...].astype(bf16)
 
 
-def invert(splits, buffer, pick):
-    pairs = splits.shape[0]
+def invert(order, buffer):
+    pairs = buffer.shape[1] // BLOCKS
     rows = 2 * pairs * 128
     return pl.pallas_call(
         invert_kernel,
@@ -98,19 +137,19 @@
             pl.BlockSpec(memory_space=pltpu.SMEM),
             pl.BlockSpec((16, BLOCKS, 16, LANES), lambda p: (0, p, 0, 0)),
             pl.BlockSpec((16, 1, 16, LANES), lambda p: (0, pairs * BLOCKS, 0, 0)),
-            pl.BlockSpec((128, LANES), lambda p: (0, 0)),
         ],
         out_specs=pl.BlockSpec((rows, LANES), lambda p: (0, 0)),
         out_shape=jax.ShapeDtypeStruct((rows, LANES), bf16),
         scratch_shapes=[pltpu.VMEM((rows, LANES), f32)],
-        compiler_params=params(),
+        compiler_params=params(60.54),
         name="invert",
-    )(splits, buffer, buffer, pick)
-
-
-def contract_kernel(split_ref, main_ref, tail_ref, order_ref, back_ref, out_ref, rows_ref):
+    )(order, buffer, buffer)
+
+
+def contract_kernel(order_ref, main_ref, tail_ref, back_ref, out_ref, rows_ref):
     p = pl.program_id(0)
-    split = split_ref[p]
+    split = own_split(order_ref, pl.num_programs(0))
+    pick = pick_matrix()
 
     @pl.when(p == 0)
     def _():
@@ -120,7 +159,7 @@
     sums = []
     for s in range(2):
         back = rows_ref[pl.ds(2 * p + s, 128, stride=2 * pl.num_programs(0)), :].astype(bf16)
-        turned = lax.dot_general(order_ref[...], back, NT, preferred_element_type=f32).astype(bf16)
+        turned = lax.dot_general(pick, back, NT, preferred_element_type=f32).astype(bf16)
         sums.append(jnp.dot(turned, data, preferred_element_type=f32))
     slot = lax.broadcasted_iota(jnp.int32, sums[0].shape, 1)
     result = jnp.where(slot < split, sums[0], sums[1])
@@ -143,8 +182,8 @@
         out_ref[:, end] = jnp.where(lane == p, last, out_ref[:, end].astype(f32)).astype(bf16)
 
 
-def contract(splits, buffer, order, back):
-    pairs = splits.shape[0]
+def contract(order, buffer, back):
+    pairs = buffer.shape[1] // BLOCKS
     out_blocks = pairs * BLOCKS // 2 + 1
     rows = 2 * pairs * 128
     return pl.pallas_call(
@@ -154,7 +193,6 @@
             pl.BlockSpec(memory_space=pltpu.SMEM),
             pl.BlockSpec((16, BLOCKS, 16, LANES), lambda p: (0, p, 0, 0)),
             pl.BlockSpec((16, 1, 16, LANES), lambda p: (0, pairs * BLOCKS, 0, 0)),
-            pl.BlockSpec((128, LANES), lambda p: (0, 0)),
             pl.BlockSpec((rows, LANES), lambda p: (0, 0)),
         ],
         out_specs=pl.BlockSpec((16, out_blocks, 16, LANES), lambda p: (0, 0, 0, 0)),
@@ -162,7 +200,7 @@
         scratch_shapes=[pltpu.VMEM((rows, LANES), f32)],
         compiler_params=params(),
         name="contract",
-    )(splits, buffer, buffer, order, back)
+    )(order, buffer, buffer, back)
 
 
 def unpack_kernel(in_ref, out_ref, rows_ref):
@@ -226,8 +264,8 @@
     return jnp.broadcast_to(row.astype(f32), (LANES, LANES)).T
 
 
-def basis_kernel(count_ref, order_ref, out_ref):
-    whole = count_ref[0].astype(f32)
+def basis_kernel(row_lat_ref, lon_count_ref, order_ref, out_ref):
+    whole = own_count(row_lat_ref, lon_count_ref).astype(f32)
     order = upright_column(order_ref[pl.ds(pl.program_id(0), 1), :])
     rows = LANES
     even = jnp.where(remainder(order, 2.0) < 0.5, order, TRUNC - order)
@@ -244,7 +282,7 @@
             out_ref[2 * kind + 1, :, at] = (sin_a * cos_fine + cos_a * sin_fine).astype(bf16)
 
 
-def basis(count, order):
+def basis(row_lat, lon_count, order):
     rows = LANES
     pairs = order.size
     return pl.pallas_call(
@@ -252,18 +290,22 @@
         grid=(pairs // rows,),
         in_specs=[
             pl.BlockSpec(memory_space=pltpu.SMEM),
+            pl.BlockSpec(memory_space=pltpu.SMEM),
             pl.BlockSpec(order.shape, lambda i: (0, 0)),
         ],
         out_specs=pl.BlockSpec((4, rows, QUARTER * LANES), lambda i: (0, i, 0)),
         out_shape=jax.ShapeDtypeStruct((4, pairs, QUARTER * LANES), bf16),
-        compiler_params=params(),
+        compiler_params=params(60),
         cost_estimate=pl.CostEstimate(flops=200_000_000, bytes_accessed=30_000_000, transcendentals=0),
         name="basis",
-    )(count, order)
-
-
-def grid_kernel(count_ref, weight_ref, order_ref, table_ref, eye_ref, in_ref, grid_ref, back_ref, place, rows_ref):
-    count = count_ref[0]
+    )(row_lat, lon_count, order)
+
+
+def grid_kernel(row_lat_ref, lon_count_ref, weight_ref, order_ref, table_hbm, in_ref, grid_ref, back_ref, place, rows_ref, table_ref, sems):
+    loads = [pltpu.make_async_copy(table_hbm.at[i], table_ref.at[i], sems.at[i]) for i in range(4)]
+    for load in loads:
+        load.start()
+    count = own_count(row_lat_ref, lon_count_ref)
     quarter = count // 4
     length = count.astype(f32)
     whole = jnp.full((1, LANES), length)
@@ -296,13 +338,19 @@
     odd_cos = jnp.where(left, coef_odd, -(coef_odd * sign_odd))
     odd_sin = -jnp.where(left, turned_odd, turned_odd * sign_odd)
 
+    eye = lax.broadcasted_iota(jnp.int32, (LANES, LANES), 0) == lax.broadcasted_iota(jnp.int32, (LANES, LANES), 1)
+    eye = jnp.where(eye, 1.0, 0.0).astype(bf16)
+
     def upright(values):
-        return lax.dot_general(eye_ref[...], values.astype(bf16), NT, preferred_element_type=f32).astype(bf16)
-
-    sum_even = jnp.dot(upright(even_cos), table_ref[0], preferred_element_type=f32)
-    sum_even += jnp.dot(upright(even_sin), table_ref[1], preferred_element_type=f32)
-    sum_odd = jnp.dot(upright(odd_cos), table_ref[2], preferred_element_type=f32)
-    sum_odd += jnp.dot(upright(odd_sin), table_ref[3], preferred_element_type=f32)
+        return lax.dot_general(eye, values.astype(bf16), NT, preferred_element_type=f32).astype(bf16)
+
+    sums = []
+    for i, values in enumerate((even_cos, even_sin, odd_cos, odd_sin)):
+        values = upright(values)
+        loads[i].wait()
+        sums.append(jnp.dot(values, table_ref[i], preferred_element_type=f32))
+    sum_even = sums[0] + sums[1]
+    sum_odd = sums[2] + sums[3]
 
     width = QUARTER * LANES
     along = lax.broadcasted_iota(jnp.int32, (1, width), 1)
@@ -327,7 +375,7 @@
             at = pl.ds(pl.multiple_of((base + b) * LANES, LANES), LANES)
             place[:, at] += merged
             before = block
-    grid_ref[...] = place[:, :WIDTH]
+    grid_ref[:, 0, :] = place[:, :WIDTH]
 
     def product(field):
         return jnp.concatenate(
@@ -350,7 +398,7 @@
     x_sin = analyse(1, both)
     y_cos = analyse(2, gap)
     y_sin = analyse(3, gap)
-    scale = weight_ref[0] * shrink
+    scale = weight_ref[own_place()[0]] * shrink
     back_even = jnp.where(
         left,
         x_cos + sign_even * pltpu.roll(x_cos, 64, 1),
@@ -368,60 +416,54 @@
     back_ref[...] = rows_ref[...].astype(bf16)
 
 
-def grid_step(count, weight, order, table, eye, coeffs):
+def grid_step(row_lat, lon_count, weights, order, table, coeffs):
     rows = 2 * order.size
     smem = pl.BlockSpec(memory_space=pltpu.SMEM)
     vmem = pl.BlockSpec(memory_space=pltpu.VMEM)
     return pl.pallas_call(
         grid_kernel,
-        in_specs=[smem, smem, vmem, vmem, vmem, vmem],
+        in_specs=[smem, smem, smem, vmem, pl.BlockSpec(memory_space=pltpu.HBM), vmem],
         out_specs=[vmem, vmem],
         out_shape=[
-            jax.ShapeDtypeStruct((64, WIDTH), f32),
+            jax.ShapeDtypeStruct((64, 1, WIDTH), f32),
             jax.ShapeDtypeStruct((rows, LANES), bf16),
         ],
         scratch_shapes=[
             pltpu.VMEM((64, (4 * QUARTER + 2) * LANES), f32),
             pltpu.VMEM((rows, LANES), f32),
-        ],
-        compiler_params=params(),
+            pltpu.VMEM(table.shape, bf16),
+            pltpu.SemaphoreType.DMA((4,)),
+        ],
+        compiler_params=params(60),
         name="grid",
-    )(count, weight, order, table, eye, coeffs)
+    )(row_lat, lon_count, weights, order, table, coeffs)
 
 
 def shards(spectral_in, legendre, weights, pair_order, row_lat, lon_count):
     band_count = lax.axis_size("band")
     lev_count = lax.axis_size("lev")
-    band_place = lax.axis_index("band")
-    lev_place = lax.axis_index("lev")
     devices = band_count * lev_count
-    pairs_dev = legendre.shape[0]
-    pairs = pairs_dev // lev_count
+    pairs = legendre.shape[0] // lev_count
     all_pairs = pair_order.shape[0]
 
-    buffer = lax.all_to_all(pack(legendre, spectral_in), "lev", 0, 0, tiled=True)
-
-    my_row = lax.dynamic_slice_in_dim(row_lat, lev_place * band_count + band_place, 1)
-    my_count = lax.dynamic_slice_in_dim(lon_count, my_row[0], 1)
-    my_weight = lax.dynamic_slice_in_dim(weights, band_place, 1)
-    my_orders = lax.dynamic_slice_in_dim(pair_order, band_place * pairs_dev + lev_place * pairs, pairs)
-    splits = TRUNC + 1 - my_orders
-    arrived = pair_order.reshape(band_count, lev_count, pairs).transpose(2, 1, 0).reshape(pairs, devices)
-    table = basis(my_count, arrived)
-
-    lane = jnp.arange(LANES, dtype=jnp.int32)
-    pick = (lane[:, None] == (2 * (lane % 64) + lane // 64)[None, :]).astype(bf16)
-    eye = (lane[:, None] == lane[None, :]).astype(bf16)
-
-    def exchange(rows):
-        rows = rows.reshape(devices, pairs, 2, LANES)
-        return lax.all_to_all(rows, ("lev", "band"), 0, 0, tiled=True).reshape(2 * all_pairs, LANES)
-
-    fourier = exchange(invert(splits, buffer, pick))
-    grid_row, back = grid_step(my_count, my_weight, arrived, table, eye, fourier)
-    spectral = contract(splits, buffer, pick, exchange(back))
-    spectral = lax.all_to_all(spectral, "lev", 0, 0, tiled=True)
-    return (grid_row.reshape(64, 1, WIDTH), unpack(spectral, pairs))
+    def exchange_pairs(blocks):
+        rows = blocks.reshape(lev_count, -1, LANES)
+        return lax.all_to_all(rows, "lev", 0, 0, tiled=True).reshape(blocks.shape)
+
+    def exchange_rows(rows):
+        rows = rows.reshape(devices, pairs, 2, LANES).transpose(0, 2, 1, 3).reshape(devices, 2, -1)
+        rows = lax.all_to_all(rows, ("lev", "band"), 0, 0, tiled=True).reshape(devices, 2, pairs, LANES)
+        return rows.transpose(0, 2, 1, 3).reshape(2 * all_pairs, LANES)
+
+    buffer = exchange_pairs(pack(legendre, spectral_in))
+    fourier = invert(pair_order, buffer)
+    fourier, arrived, row_lat, lon_count = lax.optimization_barrier((fourier, pair_order, row_lat, lon_count))
+    arrived = arrived.reshape(band_count, lev_count, pairs).transpose(2, 1, 0).reshape(pairs, devices)
+    table = basis(row_lat, lon_count, arrived)
+    fourier = exchange_rows(fourier)
+    grid_row, back = grid_step(row_lat, lon_count, weights, arrived, table, fourier)
+    spectral = exchange_pairs(contract(pair_order, buffer, exchange_rows(back)))
+    return (grid_row, unpack(spectral, pairs))
 
 
 def solution(mesh):

time: 161 us -> 143 us (0.89)
  blocking collectives: 21.1 us -> 94.8 us
  waiting for transfers between devices: 67.2 us -> 2.65 us
  starting transfers between devices: 24.7 us -> 7.78 us
  local copies, waits for them, and re-layouts: 13.6 us -> 1.79 us
  Pallas kernels: 31.4 us -> 34.8 us
  between operations: 2.79 us -> 0.68 us
    all_to_all x1 -> x3, blocking collectives: 21.1 us -> 94.8 us  [the longest x2 76 us: exchange_pairs(): return lax.all_to_all(rows, 'lev', 0, 0, tiled=True).reshape(blocks.shape)]
    all_to_all x3 -> x1, waiting for transfers between devices: 67.2 us -> 2.65 us  [exchange_rows(): lax.all_to_all(rows, ('lev', 'band'), 0, 0, tiled=True)]
    all_to_all x3 -> x1, starting transfers between devices: 24.7 us -> 7.78 us  [exchange_rows(): lax.all_to_all(rows, ('lev', 'band'), 0, 0, tiled=True)]
    unnamed x21 -> x6, local copies, waits for them, and re-layouts: 11.4 us -> 0.73 us
    dynamic_slice x3 -> x0, local copies, waits for them, and re-layouts: 1.76 us -> none  [the longest x1 0.59 us: shards(): my_weight = lax.dynamic_slice_in_dim(weights, band_place, 1)]
  transfers between devices with their start and end apart: 3 -> 1, of which waited for: 2 -> 1; matrix products, arithmetic and copies ran while one was open for 3% -> 1% of each run, Pallas kernels for 4% -> 6%
where the time goes in v3:
time: 143 us
  blocking collectives  94.8 us (66%)
  Pallas kernels  34.8 us (24%)
  starting transfers between devices  7.78 us (5%)
  waiting for transfers between devices  2.65 us (2%)
  local copies, waits for them, and re-layouts  1.79 us (1%)
    all_to_all x2, blocking collectives, exchange_pairs(): return lax.all_to_all(rows, 'lev', 0, 0, tiled=True).reshape(blocks.shape)  76 us
    all_to_all x1, blocking collectives, exchange_rows(): lax.all_to_all(rows, ('lev', 'band'), 0, 0, tiled=True)  18.8 us
    pallas_call x1, Pallas kernels, grid_step(): pl.pallas_call(grid_kernel, in_specs=[smem, smem, smem, vmem, pl.BlockSpe...  8.57 us
    pallas_call x1, Pallas kernels, basis(): pl.pallas_call(basis_kernel, grid=(pairs // rows,), in_specs=[pl.BlockSpe...  7.93 us
    all_to_all x1, starting transfers between devices, exchange_rows(): lax.all_to_all(rows, ('lev', 'band'), 0, 0, tiled=True)  7.78 us
    pallas_call x1, Pallas kernels, invert(): pl.pallas_call(invert_kernel, grid=(pairs,), in_specs=[pl.BlockSpec(memor...  6.33 us
    pallas_call x1, Pallas kernels, contract(): pl.pallas_call(contract_kernel, grid=(pairs,), in_specs=[pl.BlockSpec(mem...  4.47 us
    pallas_call x1, Pallas kernels, pack(): pl.pallas_call(pack_kernel, in_specs=[hbm, hbm], out_specs=pl.BlockSpec(m...  4.37 us
  transfers between devices with their start and end apart: 1, of which 1 were waited for; matrix products, arithmetic and copies ran while one was open for 1% of the time, Pallas kernels for 6%

profile of v3, /device:TPU:0, one launch (start us, length us, event | category | flops | bytes accessed | tf_op | source)
XLA Modules:
  0.0 142.5 jit_solution(7510753015678969417)
XLA Ops:
  0.6 4.4 %pack.1 = bf16[16,51,16,128]{3,2,1,0:T(8,128)(2,1)} custom-call(bf16[80,8,1281]{2,1,0:T(8,128)(2,1)} %leg_hbm.1, bf16[4,80,2,1281]{3,2,1,0:T(2,128)(2,1)} %spec_hbm.1), custom_call_target="tpu_custom_call" | custom-call | tf_op jit(solution)/shard_map/pack/pallas_call | solution.py:85
  5.0 49.1 %all_to_all.20 = bf16[16,816,128]{2,1,0:T(8,128)(2,1)} all-to-all(bf16[16,816,128]{2,1,0:T(8,128)(2,1)} %bitcast.32), channel_id=1, replica_groups=mesh['band'=8,'lev'=16] {'lev'}, dimensions={0} | all-to-all | bytes 6684672 | tf_op jit(solution)/shard_map/all_to_all | solution.py:451
  54.1 0.0 copy-start.1
  54.1 6.3 %invert.1 = bf16[1280,128]{1,0:T(8,128)(2,1)} custom-call(s32[640]{0:T(1024)} %order_ref.3, bf16[16,51,16,128]{3,2,1,0:T(8,128)(2,1)} %bitcast.25, bf16[16,51,16,128]{3,2,1,0:T(8,128)(2,1)} %bitcast.26), custom_call_target="tpu_custom_call" | custom-call | tf_op jit(solution)/shard_map/invert/pallas_call | solution.py:133
  60.4 7.8 %all-to-all-start.1 = ((bf16[128,2,640]{2,1,0:T(2,128)(2,1)}), bf16[128,2,640]{2,1,0:T(2,128)(2,1)S(1)}, u32[]{:S(2)}, u32[]{:S(2)}) async-start(bf16[128,2,640]{2,1,0:T(2,128)(2,1)} %bitcast.33), calls=%async_computation.1 | async-start | bytes 655360 | tf_op jit(solution)/shard_map/all_to_all | solution.py:455
  68.2 0.0 copy-done.1
  68.2 0.2 reshape.48
  68.4 0.2 copy.8
  68.6 0.7 reshape.49.order_ref
  69.3 7.9 %basis.1.table_hbm = bf16[4,640,1408]{2,1,0:T(8,128)(2,1)} custom-call(s32[128]{0:T(128)} %row_lat_ref.1, s32[128]{0:T(128)} %lon_count_ref.1, s32[5,128]{1,0:T(8,128)} %reshape.49.order_ref), custom_call_target="tpu_custom_call" | custom-call | flops 200000000 | bytes 30000000 | tf_op jit(solution)/shard_map/basis/pallas_call | solution.py:288
  77.2 2.6 %all-to-all-done.1 = bf16[128,2,640]{2,1,0:T(2,128)(2,1)S(1)} async-done(((bf16[128,2,640]{2,1,0:T(2,128)(2,1)}), bf16[128,2,640]{2,1,0:T(2,128)(2,1)S(1)}, u32[]{:S(2)}, u32[]{:S(2)}) %all-to-all-start.1) | async-done | bytes 327712 | tf_op jit(solution)/shard_map/all_to_all | solution.py:455
  79.9 0.0 copy-start.2
  79.9 0.7 copy-done.2
  80.6 0.0 copy-start
  80.6 8.6 %grid.1 = (f32[64,1,5136]{2,1,0:T(1,128)}, bf16[1280,128]{1,0:T(8,128)(2,1)}) custom-call(s32[128]{0:T(128)} %row_lat_ref.1, s32[128]{0:T(128)} %lon_count_ref.1, f32[8]{0:T(128)} %weight_ref.1, s32[5,128]{1,0:T(8,128)} %reshape.49.order_ref, bf16[4,640,1408]{2,1,0:T(8,128)(2,1)} %basis.1.table_hbm, bf16[1280,128]{1,0:T(8,128)(2,1)} %bitcast.34), custom_call_target="tpu_custom_call" | custom-call | tf_op jit(solution)/shard_map/grid/pallas_call | solution.py:423
  89.2 18.8 %all_to_all.21 = bf16[128,2,640]{2,1,0:T(2,128)(2,1)S(1)} all-to-all(bf16[128,2,640]{2,1,0:T(2,128)(2,1)} %bitcast.35), channel_id=1, replica_groups=mesh['band'=8,'lev'=16] {'lev','band'}, dimensions={0} | all-to-all | bytes 655360 | tf_op jit(solution)/shard_map/all_to_all | solution.py:455
  108.0 0.0 copy-done
  108.0 4.5 %contract.1 = bf16[16,26,16,128]{3,2,1,0:T(8,128)(2,1)S(1)} custom-call(s32[640]{0:T(1024)S(1)} %copy-done.1, bf16[16,51,16,128]{3,2,1,0:T(8,128)(2,1)S(1)} %bitcast.27, bf16[16,51,16,128]{3,2,1,0:T(8,128)(2,1)S(1)} %bitcast.28, bf16[1280,128]{1,0:T(8,128)(2,1)S(1)} %bitcast.31), custom_call_target="tpu_custom_call" | custom-call | tf_op jit(solution)/shard_map/contract/pallas_call | solution.py:189
  112.5 26.9 %all_to_all.22 = bf16[16,416,128]{2,1,0:T(8,128)(2,1)S(1)} all-to-all(bf16[16,416,128]{2,1,0:T(8,128)(2,1)S(1)} %bitcast.29), channel_id=1, replica_groups=mesh['band'=8,'lev'=16] {'lev'}, dimensions={0} | all-to-all | bytes 3407872 | tf_op jit(solution)/shard_map/all_to_all | solution.py:451
  139.4 3.1 %unpack.1 = f32[4,80,2,1281]{3,2,1,0:T(2,128)} custom-call(bf16[16,26,16,128]{3,2,1,0:T(8,128)(2,1)S(1)} %bitcast.30), custom_call_target="tpu_custom_call" | custom-call | tf_op jit(solution)/shard_map/unpack/pallas_call | solution.py:225
Async XLA Ops:
  54.1 14.1 %copy-start.1 = (s32[640]{0:T(1024)S(1)}, s32[640]{0:T(1024)}, u32[]{:S(2)}) copy-start(s32[640]{0:T(1024)} %order_ref.3) | copy-start | bytes 7684
  60.4 19.4 %all-to-all-start.1 = ((bf16[128,2,640]{2,1,0:T(2,128)(2,1)}), bf16[128,2,640]{2,1,0:T(2,128)(2,1)S(1)}, u32[]{:S(2)}, u32[]{:S(2)}) async-start(bf16[128,2,640]{2,1,0:T(2,128)(2,1)} %bitcast.33), calls=%async_computation.1 | async-start | bytes 655360 | tf_op jit(solution)/shard_map/all_to_all | solution.py:455
  79.9 0.7 copy-start.2
  80.6 27.4 %copy-start = (bf16[16,816,128]{2,1,0:T(8,128)(2,1)S(1)}, bf16[16,816,128]{2,1,0:T(8,128)(2,1)}, u32[]{:S(2)}) copy-start(bf16[16,816,128]{2,1,0:T(8,128)(2,1)} %all_to_all.20) | copy-start | bytes 10027012

commit v4 on v3

v4 whole, which is shorter than its diff:
```python
import functools
import math

import jax
import jax.numpy as jnp
from jax import lax
from jax.experimental import pallas as pl
from jax.experimental.pallas import tpu as pltpu
from jax.sharding import PartitionSpec as P

TRUNC = 1279
COEFS = TRUNC + 2
LANES = 128
BLOCKS = (COEFS - 1) // LANES
QUARTER = 11
WIDTH = 4 * TRUNC + 20

f32 = jnp.float32
bf16 = jnp.bfloat16

NT = (((1,), (1,)), ((), ()))


def params(mib=32):
    return pltpu.CompilerParams(vmem_limit_bytes=int(mib * 1024 * 1024))


def own_place():
    return lax.axis_index("band"), lax.axis_index("lev")


def own_split(order_ref, pairs, p):
    band, lev = own_place()
    return TRUNC + 1 - order_ref[(band * lax.axis_size("lev") + lev) * pairs + p]


def own_count(row_lat_ref, lon_count_ref):
    band, lev = own_place()
    return lon_count_ref[row_lat_ref[lev * lax.axis_size("band") + band]]


def pick_matrix():
    row = lax.broadcasted_iota(jnp.int32, (LANES, LANES), 0)
    lane = lax.broadcasted_iota(jnp.int32, (LANES, LANES), 1)
    return jnp.where(row == 2 * (lane % 64) + lane // 64, 1.0, 0.0).astype(bf16)


def pack_kernel(leg_hbm, spec_hbm, out_hbm, leg_ref, spec_ref, out_ref, in_sems, out_sems):
    dests = out_ref.shape[0]
    pairs = leg_ref.shape[0] // dests
    steps = in_sems.shape[0]
    size = leg_ref.shape[0] // steps
    loads, stores = [], []
    for i in range(steps):
        part = pl.ds(i * size, size)
        loads.append(
            (
                pltpu.make_async_copy(leg_hbm.at[part], leg_ref.at[part], in_sems.at[i, 0]),
                pltpu.make_async_copy(spec_hbm.at[:, part], spec_ref.at[:, part], in_sems.at[i, 1]),
            )
        )
        part = pl.ds(i * (dests // steps), dests // steps)
        stores.append(pltpu.make_async_copy(out_ref.at[part], out_hbm.at[part], out_sems.at[i]))
    for pair in loads:
        for copy in pair:
            copy.start()
    lane = lax.broadcasted_iota(jnp.int32, (16, LANES), 1)
    for i in range(steps):
        for copy in loads[i]:
            copy.wait()
        for d in range(i * (dests // steps), (i + 1) * (dests // steps)):
            tail = jnp.zeros((16, LANES), f32)
            for p in range(pairs):
                at = d * pairs + p
                table = leg_ref[at].astype(f32)
                spec = jnp.concatenate([spec_ref[l, at].astype(f32) for l in range(4)], axis=0)
                rows = jnp.concatenate([table, spec], axis=0)
                for b in range(BLOCKS):
                    out_ref[d, p * BLOCKS + b] = rows[:, b * LANES : (b + 1) * LANES].astype(bf16)
                tail = jnp.where(lane == p, rows[:, COEFS - 1 : COEFS], tail)
            out_ref[d, pairs * BLOCKS] = tail.astype(bf16)
        stores[i].start()
    for store in stores:
        store.wait()


def pack(legendre, spectral):
    pairs = legendre.shape[0] // 16
    out = jax.ShapeDtypeStruct((16, pairs * BLOCKS + 1, 16, LANES), bf16)
    hbm = pl.BlockSpec(memory_space=pltpu.HBM)
    return pl.pallas_call(
        pack_kernel,
        in_specs=[hbm, hbm],
        out_specs=hbm,
        out_shape=out,
        scratch_shapes=[
            pltpu.VMEM(legendre.shape, bf16),
            pltpu.VMEM(spectral.shape, bf16),
            pltpu.VMEM(out.shape, bf16),
            pltpu.SemaphoreType.DMA((8, 2)),
            pltpu.SemaphoreType.DMA((8,)),
        ],
        compiler_params=params(60),
        name="pack",
    )(legendre, spectral)


def halves(buffer_ref, p, which):
    end = buffer_ref.shape[1] - 1
    parts = [buffer_ref[:, p * BLOCKS + b] for b in range(BLOCKS)] + [buffer_ref[:, end]]
    first = which * 8
    return jnp.concatenate(
        [part.astype(f32)[:, first : first + 8].reshape(128, LANES).astype(bf16) for part in parts], axis=1
    )


def invert_kernel(order_ref, buffer_ref, out_ref, rows_ref):
    pairs = buffer_ref.shape[1] // BLOCKS
    pick = pick_matrix()
    whole = BLOCKS * LANES
    for p in range(pairs):
        split = own_split(order_ref, pairs, p)
        table = halves(buffer_ref, p, 0)
        data = halves(buffer_ref, p, 1)
        slot = lax.broadcasted_iota(jnp.int32, (16, data.shape[1]), 1)
        first = (slot < split) & (slot < whole)
        second = ((slot >= split) & (slot < whole)) | (slot == whole + p)
        apart = data.reshape(8, 16, data.shape[1])
        kept = [(apart * jnp.where(part, 1.0, 0.0).astype(bf16)[None]).reshape(data.shape) for part in (first, second)]
        sums = lax.dot_general(table, jnp.concatenate(kept, axis=0), NT, preferred_element_type=f32).astype(bf16)
        for s in range(2):
            part = jnp.dot(sums[:, s * LANES : (s + 1) * LANES], pick, preferred_element_type=f32)
            rows_ref[pl.ds(2 * p + s, 128, stride=2 * pairs), :] = part
    out_ref[...] = rows_ref[...].astype(bf16)


def invert(order, buffer):
    pairs = buffer.shape[1] // BLOCKS
    rows = 2 * pairs * 128
    vmem = pl.BlockSpec(memory_space=pltpu.VMEM)
    return pl.pallas_call(
        invert_kernel,
        in_specs=[pl.BlockSpec(memory_space=pltpu.SMEM), vmem],
        out_specs=vmem,
        out_shape=jax.ShapeDtypeStruct((rows, LANES), bf16),
        scratch_shapes=[pltpu.VMEM((rows, LANES), f32)],
        compiler_params=params(),
        name="invert",
    )(order, buffer)


def contract_kernel(order_ref, buffer_ref, back_ref, out_ref, rows_ref):
    pairs = buffer_ref.shape[1] // BLOCKS
    pick = pick_matrix()
    rows_ref[...] = back_ref[...].astype(f32)
    lane = lax.broadcasted_iota(jnp.int32, (LANES, LANES), 1)
    end = jnp.zeros((LANES, LANES), f32)
    for p in range(pairs):
        split = own_split(order_ref, pairs, p)
        data = halves(buffer_ref, p, 0)
        turned = []
        for s in range(2):
            back = rows_ref[pl.ds(2 * p + s, 128, stride=2 * pairs), :].astype(bf16)
            turned.append(lax.dot_general(pick, back, NT, preferred_element_type=f32).astype(bf16))
        sums = jnp.dot(jnp.concatenate(turned, axis=0), data, preferred_element_type=f32)
        slot = lax.broadcasted_iota(jnp.int32, (LANES, data.shape[1]), 1)
        result = jnp.where(slot < split, sums[:LANES], sums[LANES:])
        for b in range(0, BLOCKS, 2):
            left = result[:, b * LANES : (b + 1) * LANES].reshape(16, 8, LANES)
            right = result[:, (b + 1) * LANES : (b + 2) * LANES].reshape(16, 8, LANES)
            out_ref[:, p * (BLOCKS // 2) + b // 2] = jnp.concatenate([left, right], axis=1).astype(bf16)
        end = jnp.where(lane == p, sums[LANES:, BLOCKS * LANES :], end)
    end = end.reshape(16, 8, LANES)
    out_ref[:, pairs * (BLOCKS // 2)] = jnp.concatenate([end, end], axis=1).astype(bf16)


def contract(order, buffer, back):
    pairs = buffer.shape[1] // BLOCKS
    out_blocks = pairs * BLOCKS // 2 + 1
    vmem = pl.BlockSpec(memory_space=pltpu.VMEM)
    return pl.pallas_call(
        contract_kernel,
        in_specs=[pl.BlockSpec(memory_space=pltpu.SMEM), vmem, vmem],
        out_specs=vmem,
        out_shape=jax.ShapeDtypeStruct((16, out_blocks, 16, LANES), bf16),
        scratch_shapes=[pltpu.VMEM((2 * pairs * 128, LANES), f32)],
        compiler_params=params(),
        name="contract",
    )(order, buffer, back)


def unpack_kernel(in_ref, out_hbm, rows_ref, out_ref, sems):
    senders = in_ref.shape[0]
    pairs = out_ref.shape[1] // senders
    blocks = in_ref.shape[1]
    steps = sems.shape[0]
    stores = []
    for i in range(steps):
        part = pl.ds(i * (senders // steps) * pairs, (senders // steps) * pairs)
        stores.append(pltpu.make_async_copy(out_ref.at[:, part], out_hbm.at[:, part], sems.at[i]))
    for d in range(senders):
        rows = rows_ref.at[d % 2]
        rows[...] = in_ref[d].astype(f32)
        for p in range(pairs):
            for b in range(BLOCKS):
                for l in range(4):
                    pair = rows[p * (BLOCKS // 2) + b // 2, pl.ds(b % 2 * 8 + 2 * l, 2), :]
                    out_ref[l, d * pairs + p, :, b * LANES : (b + 1) * LANES] = pair
            for l in range(4):
                last = rows[blocks - 1, pl.ds(2 * l, 2), :]
                out_ref[l, d * pairs + p, :, COEFS - 1 : COEFS] = last[:, p : p + 1]
        if (d + 1) % (senders // steps) == 0:
            stores[d // (senders // steps)].start()
    for store in stores:
        store.wait()


def unpack(buffer, pairs):
    blocks = buffer.shape[1]
    out = jax.ShapeDtypeStruct((4, 16 * pairs, 2, COEFS), f32)
    return pl.pallas_call(
        unpack_kernel,
        in_specs=[pl.BlockSpec(memory_space=pltpu.VMEM)],
        out_specs=pl.BlockSpec(memory_space=pltpu.HBM),
        out_shape=out,
        scratch_shapes=[
            pltpu.VMEM((2, blocks, 16, LANES), f32),
            pltpu.VMEM(out.shape, f32),
            pltpu.SemaphoreType.DMA((8,)),
        ],
        compiler_params=params(),
        name="unpack",
    )(buffer)


def turn(whole, part):
    scaled = part * (4.0 / whole)
    nearest = jnp.floor(scaled + 0.5)
    angle = (scaled - nearest) * (math.pi / 2)
    square = angle * angle
    sine = angle + angle * square * (
        -1.6666654611e-1 + square * (8.3321608736e-3 - 1.9515295891e-4 * square)
    )
    cosine = 1.0 - 0.5 * square + square * square * (
        4.166664568298827e-2 + square * (-1.388731625493765e-3 + 2.443315711809948e-5 * square)
    )
    odd = (nearest == 1.0) | (nearest == 3.0)
    cos_base = jnp.where(odd, sine, cosine)
    sin_base = jnp.where(odd, cosine, sine)
    cos_sign = jnp.where((nearest == 1.0) | (nearest == 2.0), -1.0, 1.0)
    sin_sign = jnp.where((nearest == 2.0) | (nearest == 3.0), -1.0, 1.0)
    return cos_base * cos_sign, sin_base * sin_sign


def remainder(value, whole):
    quotient = jnp.floor(value * (1.0 / whole))
    rest = value - quotient * whole
    rest = jnp.where(rest < 0.0, rest + whole, rest)
    return jnp.where(rest >= whole, rest - whole, rest)


def upright_column(row):
    return jnp.broadcast_to(row.astype(f32), (LANES, LANES)).T


def basis_kernel(row_lat_ref, lon_count_ref, order_ref, out_ref):
    whole = own_count(row_lat_ref, lon_count_ref).astype(f32)
    order = upright_column(order_ref[pl.ds(pl.program_id(0), 1), :])
    wave = jnp.where(remainder(order, 2.0) < 0.5, order, TRUNC - order)
    lane = lax.broadcasted_iota(jnp.int32, (LANES, LANES), 1).astype(f32)
    cos_fine, sin_fine = turn(whole, remainder(wave * lane, whole))
    cos_coarse, sin_coarse = turn(whole, remainder(wave * (lane * 128.0), whole))
    for a in range(QUARTER):
        cos_a = cos_coarse[:, a : a + 1]
        sin_a = sin_coarse[:, a : a + 1]
        at = pl.ds(a * LANES, LANES)
        out_ref[0, :, at] = (cos_a * cos_fine - sin_a * sin_fine).astype(bf16)
        out_ref[1, :, at] = (sin_a * cos_fine + cos_a * sin_fine).astype(bf16)


def basis(row_lat, lon_count, order):
    rows = LANES
    pairs = order.size
    return pl.pallas_call(
        basis_kernel,
        grid=(pairs // rows,),
        in_specs=[
            pl.BlockSpec(memory_space=pltpu.SMEM),
            pl.BlockSpec(memory_space=pltpu.SMEM),
            pl.BlockSpec(order.shape, lambda i: (0, 0)),
        ],
        out_specs=pl.BlockSpec((2, rows, QUARTER * LANES), lambda i: (0, i, 0)),
        out_shape=jax.ShapeDtypeStruct((2, pairs, QUARTER * LANES), bf16),
        compiler_params=params(60),
        cost_estimate=pl.CostEstimate(flops=200_000_000, bytes_accessed=30_000_000, transcendentals=0),
        name="basis",
    )(row_lat, lon_count, order)


def grid_kernel(row_lat_ref, lon_count_ref, weight_ref, order_ref, table_hbm, in_ref, grid_hbm, back_ref, place, rows_ref, table_ref, grid_ref, sems):
    loads = [pltpu.make_async_copy(table_hbm.at[i], table_ref.at[i], sems.at[i]) for i in range(2)]
    leave = pltpu.make_async_copy(grid_ref, grid_hbm, sems.at[2])
    for load in loads:
        load.start()
    count = own_count(row_lat_ref, lon_count_ref)
    quarter = count // 4
    length = count.astype(f32)
    whole = jnp.full((1, LANES), length)
    shrink = lax.rsqrt(whole)
    groups = order_ref.shape[0]
    pairs = groups * LANES
    order = jnp.concatenate([upright_column(order_ref[pl.ds(i, 1), :]) for i in range(groups)], axis=0)
    swap = remainder(order, 2.0) < 0.5
    even = jnp.where(swap, order, TRUNC - order)
    odd = TRUNC - even
    left = lax.broadcasted_iota(jnp.int32, (pairs, LANES), 1) < 64
    sign_even = jnp.where(remainder(even, 4.0) < 0.5, 1.0, -1.0)
    keep_even = jnp.where(2.0 * even < length, jnp.where(even < 0.5, 1.0, 2.0), 0.0)
    keep_odd = jnp.where(2.0 * odd < length, 2.0, 0.0)
    rows_ref[...] = in_ref[...].astype(f32)

    def arrived(s):
        parts = [rows_ref[pl.ds(2 * i + s, LANES, stride=2 * groups), :] for i in range(groups)]
        return jnp.concatenate(parts, axis=0)

    first = arrived(0)
    second = arrived(1)
    coef_even = jnp.where(swap, first, second) * keep_even
    coef_odd = jnp.where(swap, second, first) * keep_odd
    turned_even = pltpu.roll(coef_even, 64, 1)
    turned_odd = pltpu.roll(coef_odd, 64, 1)
    even_cos = jnp.where(left, coef_even, turned_even * sign_even)
    even_sin = -jnp.where(left, turned_even, coef_even * sign_even)
    odd_cos = jnp.where(left, coef_odd, -coef_odd)
    odd_sin = turned_odd

    eye = lax.broadcasted_iota(jnp.int32, (LANES, LANES), 0) == lax.broadcasted_iota(jnp.int32, (LANES, LANES), 1)
    eye = jnp.where(eye, 1.0, 0.0).astype(bf16)

    def upright(values):
        return lax.dot_general(eye, values.astype(bf16), NT, preferred_element_type=f32).astype(bf16)

    waves = (
        (even_cos, odd_cos, odd_cos * sign_even),
        (even_sin, odd_sin, odd_sin * sign_even),
    )
    sums = 0.0
    for i in range(2):
        values = jnp.concatenate([upright(wave) for wave in waves[i]], axis=0)
        loads[i].wait()
        sums += jnp.dot(values, table_ref[i], preferred_element_type=f32)

    width = QUARTER * LANES
    along = lax.broadcasted_iota(jnp.int32, (1, width), 1)
    factor = jnp.where(along < quarter, jnp.broadcast_to(shrink[:, :1], (1, width)), 0.0)
    place_along = along.astype(f32)
    cos_phase, sin_phase = turn(length, remainder(place_along * float(TRUNC), length))
    sum_even = sums[:128]
    sum_odd = jnp.concatenate(
        [
            cos_phase * sums[128:192] + sin_phase * sums[192:256],
            sin_phase * sums[256:320] - cos_phase * sums[320:],
        ],
        axis=0,
    )
    near = (sum_even + sum_odd) * factor
    far = (sum_even - sum_odd) * factor

    place[...] = jnp.zeros_like(place)
    narrow = lax.broadcasted_iota(jnp.int32, (64, LANES), 1)
    for t, field in enumerate((near[:64], near[64:], far[:64], far[64:])):
        start = t * quarter
        shift = start % LANES
        base = start // LANES
        before = jnp.zeros((64, LANES), f32)
        for b in range(QUARTER + 1):
            if b < QUARTER:
                block = field[:, b * LANES : (b + 1) * LANES]
                block = pltpu.roll(block, shift, 1)
            else:
                block = jnp.zeros((64, LANES), f32)
            merged = jnp.where(narrow < shift, before, block)
            at = pl.ds(pl.multiple_of((base + b) * LANES, LANES), LANES)
            place[:, at] += merged
            before = block
    grid_ref[:, 0, :] = place[:, :WIDTH]
    leave.start()

    def product(field):
        return jnp.concatenate(
            [
                half * jnp.concatenate([half[1:], half[:1]], axis=0)
                for half in (field[:64], field[64:])
            ],
            axis=0,
        )

    near = product(near)
    far = product(far)
    both = near + far
    gap = near - far
    first_cos, first_sin = cos_phase * gap[:64], sin_phase * gap[:64]
    second_cos, second_sin = cos_phase * gap[64:], sin_phase * gap[64:]

    def analyse(index, *parts):
        parts = jnp.concatenate(parts, axis=0).astype(bf16)
        return lax.dot_general(table_ref[index], parts, NT, preferred_element_type=f32)

    by_cos = analyse(0, both, first_cos, -first_sin, second_sin, second_cos)
    by_sin = analyse(1, both, first_sin, first_cos, -second_cos, second_sin)
    x_cos, x_sin = by_cos[:, :LANES], by_sin[:, :LANES]
    y_plain = by_cos[:, LANES : 2 * LANES] + by_sin[:, LANES : 2 * LANES]
    y_signed = by_cos[:, 2 * LANES :] + by_sin[:, 2 * LANES :]
    scale = weight_ref[own_place()[0]] * shrink
    back_even = jnp.where(
        left,
        x_cos + sign_even * pltpu.roll(x_cos, 64, 1),
        -(sign_even * x_sin + pltpu.roll(x_sin, 64, 1)),
    )
    back_odd = y_plain + sign_even * y_signed
    back_even = jnp.where(keep_even > 0.0, back_even * scale, 0.0)
    back_odd = jnp.where(keep_odd > 0.0, back_odd * scale, 0.0)
    leaving = (jnp.where(swap, back_even, back_odd), jnp.where(swap, back_odd, back_even))
    for s in range(2):
        for i in range(groups):
            part = leaving[s][i * LANES : (i + 1) * LANES]
            rows_ref[pl.ds(2 * i + s, LANES, stride=2 * groups), :] = part
    back_ref[...] = rows_ref[...].astype(bf16)
    leave.wait()


def grid_step(row_lat, lon_count, weights, order, table, coeffs):
    rows = 2 * order.size
    smem = pl.BlockSpec(memory_space=pltpu.SMEM)
    vmem = pl.BlockSpec(memory_space=pltpu.VMEM)
    return pl.pallas_call(
        grid_kernel,
        in_specs=[smem, smem, smem, vmem, pl.BlockSpec(memory_space=pltpu.HBM), vmem],
        out_specs=[pl.BlockSpec(memory_space=pltpu.HBM), vmem],
        out_shape=[
            jax.ShapeDtypeStruct((64, 1, WIDTH), f32),
            jax.ShapeDtypeStruct((rows, LANES), bf16),
        ],
        scratch_shapes=[
            pltpu.VMEM((64, (4 * QUARTER + 2) * LANES), f32),
            pltpu.VMEM((rows, LANES), f32),
            pltpu.VMEM(table.shape, bf16),
            pltpu.VMEM((64, 1, WIDTH), f32),
            pltpu.SemaphoreType.DMA((3,)),
        ],
        compiler_params=params(60),
        name="grid",
    )(row_lat, lon_count, weights, order, table, coeffs)


def shards(spectral_in, legendre, weights, pair_order, row_lat, lon_count):
    band_count = lax.axis_size("band")
    lev_count = lax.axis_size("lev")
    devices = band_count * lev_count
    pairs = legendre.shape[0] // lev_count
    all_pairs = pair_order.shape[0]

    def exchange_pairs(blocks):
        rows = blocks.reshape(lev_count, -1, LANES)
        return lax.all_to_all(rows, "lev", 0, 0, tiled=True).reshape(blocks.shape)

    def exchange_rows(rows):
        rows = rows.reshape(devices, pairs, 2, LANES).transpose(0, 2, 1, 3).reshape(devices, 2, -1)
        rows = lax.all_to_all(rows, ("lev", "band"), 0, 0, tiled=True).reshape(devices, 2, pairs, LANES)
        return rows.transpose(0, 2, 1, 3).reshape(2 * all_pairs, LANES)

    buffer = exchange_pairs(pack(legendre, spectral_in))
    fourier = invert(pair_order, buffer)
    fourier, arrived, row_lat, lon_count = lax.optimization_barrier((fourier, pair_order, row_lat, lon_count))
    arrived = arrived.reshape(band_count, lev_count, pairs).transpose(2, 1, 0).reshape(pairs, devices)
    table = basis(row_lat, lon_count, arrived)
    fourier = exchange_rows(fourier)
    grid_row, back = grid_step(row_lat, lon_count, weights, arrived, table, fourier)
    spectral = exchange_pairs(contract(pair_order, buffer, exchange_rows(back)))
    return (grid_row, unpack(spectral, pairs))


def solution(mesh):
    return jax.shard_map(
        shards,
        mesh=mesh,
        in_specs=(P("lev", "band", None, None), P("band", "lev", None), P("lev"), P(), P(), P()),
        out_specs=(P(None, ("lev", "band"), None), P("lev", "band", None, None)),
        check_vma=False,
    )
```

time: 143 us -> 133 us (0.930)
  Pallas kernels: 34.8 us -> 24.8 us
  blocking collectives: 94.8 us -> 92.4 us
  waiting for transfers between devices: 2.65 us -> 4.91 us
    pallas_call x4, Pallas kernels: 18.3 us -> 11.4 us  [the longest x1 3.47 us: pack(): pl.pallas_call(pack_kernel, in_specs=[hbm, hbm], out_specs=hbm, out_shape...]
    pallas_call x1, Pallas kernels: 7.93 us -> 5.3 us  [basis(): pl.pallas_call(basis_kernel, grid=(pairs // rows,), in_specs=[pl.BlockSpe...]
    all_to_all x1, blocking collectives: 18.8 us -> 16.5 us  [exchange_rows(): lax.all_to_all(rows, ('lev', 'band'), 0, 0, tiled=True)]
    all_to_all x1, waiting for transfers between devices: 2.65 us -> 4.91 us  [exchange_rows(): lax.all_to_all(rows, ('lev', 'band'), 0, 0, tiled=True)]
  transfers between devices with their start and end apart: 1 -> 1, of which waited for: 1 -> 1; matrix products, arithmetic and copies ran while one was open for 1% -> 1% of each run, Pallas kernels for 6% -> 4%
where the time goes in v4:
time: 133 us
  blocking collectives  92.4 us (69%)
  Pallas kernels  24.8 us (19%)
  starting transfers between devices  8.25 us (6%)
  waiting for transfers between devices  4.91 us (4%)
  local copies, waits for them, and re-layouts  1.8 us (1%)
    all_to_all x2, blocking collectives, exchange_pairs(): return lax.all_to_all(rows, 'lev', 0, 0, tiled=True).reshape(blocks.shape)  75.9 us
    all_to_all x1, blocking collectives, exchange_rows(): lax.all_to_all(rows, ('lev', 'band'), 0, 0, tiled=True)  16.5 us
    all_to_all x1, starting transfers between devices, exchange_rows(): lax.all_to_all(rows, ('lev', 'band'), 0, 0, tiled=True)  8.25 us
    pallas_call x1, Pallas kernels, grid_step(): pl.pallas_call(grid_kernel, in_specs=[smem, smem, smem, vmem, pl.BlockSpe...  8.13 us
    pallas_call x1, Pallas kernels, basis(): pl.pallas_call(basis_kernel, grid=(pairs // rows,), in_specs=[pl.BlockSpe...  5.3 us
    all_to_all x1, waiting for transfers between devices, exchange_rows(): lax.all_to_all(rows, ('lev', 'band'), 0, 0, tiled=True)  4.91 us
    pallas_call x1, Pallas kernels, pack(): pl.pallas_call(pack_kernel, in_specs=[hbm, hbm], out_specs=hbm, out_shape...  3.47 us
    pallas_call x1, Pallas kernels, invert(): pl.pallas_call(invert_kernel, in_specs=[pl.BlockSpec(memory_space=pltpu.S...  2.96 us
  transfers between devices with their start and end apart: 1, of which 1 were waited for; matrix products, arithmetic and copies ran while one was open for 1% of the time, Pallas kernels for 4%

profile of v4, /device:TPU:0, one launch (start us, length us, event | category | flops | bytes accessed | tf_op | source)
XLA Modules:
  0.0 132.9 jit_solution(8614970822236607271)
XLA Ops:
  0.6 3.5 %pack.1 = bf16[16,51,16,128]{3,2,1,0:T(8,128)(2,1)} custom-call(bf16[80,8,1281]{2,1,0:T(8,128)(2,1)} %leg_hbm.1, bf16[4,80,2,1281]{3,2,1,0:T(2,128)(2,1)} %spec_hbm.1), custom_call_target="tpu_custom_call" | custom-call | tf_op jit(solution)/shard_map/pack/pallas_call | solution.py:91
  4.1 0.0 copy-start.1
  4.1 49.0 %all_to_all.20 = bf16[16,816,128]{2,1,0:T(8,128)(2,1)S(1)} all-to-all(bf16[16,816,128]{2,1,0:T(8,128)(2,1)} %bitcast.31), channel_id=1, replica_groups=mesh['band'=8,'lev'=16] {'lev'}, dimensions={0} | all-to-all | bytes 6684672 | tf_op jit(solution)/shard_map/all_to_all | solution.py:465
  53.1 0.0 copy-done.1
  53.1 3.0 %invert.1 = bf16[1280,128]{1,0:T(8,128)(2,1)S(1)} custom-call(s32[640]{0:T(1024)S(1)} %copy-done.1, bf16[16,51,16,128]{3,2,1,0:T(8,128)(2,1)S(1)} %bitcast.25), custom_call_target="tpu_custom_call" | custom-call | tf_op jit(solution)/shard_map/invert/pallas_call | solution.py:141
  56.1 0.0 copy-start
  56.1 0.7 copy-done
  56.8 8.3 %all-to-all-start.1 = ((bf16[128,2,640]{2,1,0:T(2,128)(2,1)}), bf16[128,2,640]{2,1,0:T(2,128)(2,1)}, u32[]{:S(2)}, u32[]{:S(2)}) async-start(bf16[128,2,640]{2,1,0:T(2,128)(2,1)} %bitcast.30), calls=%async_computation.1 | async-start | bytes 655360 | tf_op jit(solution)/shard_map/all_to_all | solution.py:469
  65.1 0.2 reshape.48
  65.3 0.2 copy.8
  65.5 0.7 reshape.49.order_ref
  66.2 5.3 %basis.1.table_hbm = bf16[2,640,1408]{2,1,0:T(8,128)(2,1)} custom-call(s32[128]{0:T(128)} %row_lat_ref.1, s32[128]{0:T(128)} %lon_count_ref.1, s32[5,128]{1,0:T(8,128)} %reshape.49.order_ref), custom_call_target="tpu_custom_call" | custom-call | flops 200000000 | bytes 30000000 | tf_op jit(solution)/shard_map/basis/pallas_call | solution.py:284
  71.4 4.9 %all-to-all-done.1 = bf16[128,2,640]{2,1,0:T(2,128)(2,1)} async-done(((bf16[128,2,640]{2,1,0:T(2,128)(2,1)}), bf16[128,2,640]{2,1,0:T(2,128)(2,1)}, u32[]{:S(2)}, u32[]{:S(2)}) %all-to-all-start.1) | async-done | bytes 327712 | tf_op jit(solution)/shard_map/all_to_all | solution.py:469
  76.4 8.1 %grid.1 = (f32[64,1,5136]{2,1,0:T(1,128)}, bf16[1280,128]{1,0:T(8,128)(2,1)}) custom-call(s32[128]{0:T(128)} %row_lat_ref.1, s32[128]{0:T(128)} %lon_count_ref.1, f32[8]{0:T(128)} %weight_ref.1, s32[5,128]{1,0:T(8,128)} %reshape.49.order_ref, bf16[2,640,1408]{2,1,0:T(8,128)(2,1)} %basis.1.table_hbm, bf16[1280,128]{1,0:T(8,128)(2,1)} %bitcast.8.in_ref), custom_call_target="tpu_custom_call" | custom-call | tf_op jit(solution)/shard_map/grid/pallas_call | solution.py:436
  84.5 16.5 %all_to_all.21 = bf16[128,2,640]{2,1,0:T(2,128)(2,1)S(1)} all-to-all(bf16[128,2,640]{2,1,0:T(2,128)(2,1)} %bitcast.32), channel_id=1, replica_groups=mesh['band'=8,'lev'=16] {'lev','band'}, dimensions={0} | all-to-all | bytes 655360 | tf_op jit(solution)/shard_map/all_to_all | solution.py:469
  101.0 2.3 %contract.1 = bf16[16,26,16,128]{3,2,1,0:T(8,128)(2,1)S(1)} custom-call(s32[640]{0:T(1024)S(1)} %copy-done.1, bf16[16,51,16,128]{3,2,1,0:T(8,128)(2,1)S(1)} %bitcast.26, bf16[1280,128]{1,0:T(8,128)(2,1)S(1)} %bitcast.29), custom_call_target="tpu_custom_call" | custom-call | tf_op jit(solution)/shard_map/contract/pallas_call | solution.py:181
  103.4 26.9 %all_to_all.22 = bf16[16,416,128]{2,1,0:T(8,128)(2,1)S(1)} all-to-all(bf16[16,416,128]{2,1,0:T(8,128)(2,1)S(1)} %bitcast.27), channel_id=1, replica_groups=mesh['band'=8,'lev'=16] {'lev'}, dimensions={0} | all-to-all | bytes 3407872 | tf_op jit(solution)/shard_map/all_to_all | solution.py:465
  130.3 2.6 %unpack.1 = f32[4,80,2,1281]{3,2,1,0:T(2,128)} custom-call(bf16[16,26,16,128]{3,2,1,0:T(8,128)(2,1)S(1)} %bitcast.28), custom_call_target="tpu_custom_call" | custom-call | tf_op jit(solution)/shard_map/unpack/pallas_call | solution.py:221
Async XLA Ops:
  4.1 49.0 %copy-start.1 = (s32[640]{0:T(1024)S(1)}, s32[640]{0:T(1024)}, u32[]{:S(2)}) copy-start(s32[640]{0:T(1024)} %order_ref.3) | copy-start | bytes 7684
  56.1 0.7 copy-start
  56.8 19.5 %all-to-all-start.1 = ((bf16[128,2,640]{2,1,0:T(2,128)(2,1)}), bf16[128,2,640]{2,1,0:T(2,128)(2,1)}, u32[]{:S(2)}, u32[]{:S(2)}) async-start(bf16[128,2,640]{2,1,0:T(2,128)(2,1)} %bitcast.30), calls=%async_computation.1 | async-start | bytes 655360 | tf_op jit(solution)/shard_map/all_to_all | solution.py:469

commit v5 on v4

--- a/solution.py
+++ b/solution.py
@@ -59,7 +59,7 @@
                 pltpu.make_async_copy(spec_hbm.at[:, part], spec_ref.at[:, part], in_sems.at[i, 1]),
             )
         )
-        part = pl.ds(i * (dests // steps), dests // steps)
+        part = pl.ds(dests - (i + 1) * (dests // steps), dests // steps)
         stores.append(pltpu.make_async_copy(out_ref.at[part], out_hbm.at[part], out_sems.at[i]))
     for pair in loads:
         for copy in pair:
@@ -76,9 +76,9 @@
                 spec = jnp.concatenate([spec_ref[l, at].astype(f32) for l in range(4)], axis=0)
                 rows = jnp.concatenate([table, spec], axis=0)
                 for b in range(BLOCKS):
-                    out_ref[d, p * BLOCKS + b] = rows[:, b * LANES : (b + 1) * LANES].astype(bf16)
+                    out_ref[dests - 1 - d, p * BLOCKS + b] = rows[:, b * LANES : (b + 1) * LANES].astype(bf16)
                 tail = jnp.where(lane == p, rows[:, COEFS - 1 : COEFS], tail)
-            out_ref[d, pairs * BLOCKS] = tail.astype(bf16)
+            out_ref[dests - 1 - d, pairs * BLOCKS] = tail.astype(bf16)
         stores[i].start()
     for store in stores:
         store.wait()
@@ -109,14 +109,16 @@
     end = buffer_ref.shape[1] - 1
     parts = [buffer_ref[:, p * BLOCKS + b] for b in range(BLOCKS)] + [buffer_ref[:, end]]
     first = which * 8
-    return jnp.concatenate(
-        [part.astype(f32)[:, first : first + 8].reshape(128, LANES).astype(bf16) for part in parts], axis=1
-    )
+
+    def rows(part):
+        part = part.astype(f32)[:, first : first + 8]
+        return jnp.concatenate([part[d] for d in reversed(range(part.shape[0]))], axis=0).astype(bf16)
+
+    return jnp.concatenate([rows(part) for part in parts], axis=1)
 
 
 def invert_kernel(order_ref, buffer_ref, out_ref, rows_ref):
     pairs = buffer_ref.shape[1] // BLOCKS
-    pick = pick_matrix()
     whole = BLOCKS * LANES
     for p in range(pairs):
         split = own_split(order_ref, pairs, p)
@@ -127,11 +129,11 @@
         second = ((slot >= split) & (slot < whole)) | (slot == whole + p)
         apart = data.reshape(8, 16, data.shape[1])
         kept = [(apart * jnp.where(part, 1.0, 0.0).astype(bf16)[None]).reshape(data.shape) for part in (first, second)]
-        sums = lax.dot_general(table, jnp.concatenate(kept, axis=0), NT, preferred_element_type=f32).astype(bf16)
+        sums = lax.dot_general(table, jnp.concatenate(kept, axis=0), NT, preferred_element_type=f32)
         for s in range(2):
-            part = jnp.dot(sums[:, s * LANES : (s + 1) * LANES], pick, preferred_element_type=f32)
-            rows_ref[pl.ds(2 * p + s, 128, stride=2 * pairs), :] = part
-    out_ref[...] = rows_ref[...].astype(bf16)
+            rows_ref[pl.ds(2 * p + s, 128, stride=2 * pairs), :] = sums[:, s * LANES : (s + 1) * LANES]
+    rows = rows_ref[...].astype(bf16)
+    out_ref[...] = jnp.dot(rows, pick_matrix(), preferred_element_type=f32).astype(bf16)
 
 
 def invert(order, buffer):
@@ -151,27 +153,31 @@
 
 def contract_kernel(order_ref, buffer_ref, back_ref, out_ref, rows_ref):
     pairs = buffer_ref.shape[1] // BLOCKS
-    pick = pick_matrix()
     rows_ref[...] = back_ref[...].astype(f32)
+    apart = [rows_ref[pl.ds(i, 128, stride=2 * pairs), :] for i in range(2 * pairs)]
+    apart = jnp.concatenate(apart, axis=0).astype(bf16)
+    turned = lax.dot_general(pick_matrix(), apart, NT, preferred_element_type=f32).astype(bf16)
     lane = lax.broadcasted_iota(jnp.int32, (LANES, LANES), 1)
     end = jnp.zeros((LANES, LANES), f32)
     for p in range(pairs):
         split = own_split(order_ref, pairs, p)
         data = halves(buffer_ref, p, 0)
-        turned = []
-        for s in range(2):
-            back = rows_ref[pl.ds(2 * p + s, 128, stride=2 * pairs), :].astype(bf16)
-            turned.append(lax.dot_general(pick, back, NT, preferred_element_type=f32).astype(bf16))
-        sums = jnp.dot(jnp.concatenate(turned, axis=0), data, preferred_element_type=f32)
+        at = 2 * p * LANES
+        back = jnp.concatenate([turned[:, at : at + LANES], turned[:, at + LANES : at + 2 * LANES]], axis=0)
+        sums = jnp.dot(back, data, preferred_element_type=f32)
         slot = lax.broadcasted_iota(jnp.int32, (LANES, data.shape[1]), 1)
         result = jnp.where(slot < split, sums[:LANES], sums[LANES:])
         for b in range(0, BLOCKS, 2):
-            left = result[:, b * LANES : (b + 1) * LANES].reshape(16, 8, LANES)
-            right = result[:, (b + 1) * LANES : (b + 2) * LANES].reshape(16, 8, LANES)
-            out_ref[:, p * (BLOCKS // 2) + b // 2] = jnp.concatenate([left, right], axis=1).astype(bf16)
+            for d in range(16):
+                at = slice(d * 8, (d + 1) * 8)
+                left = result[at, b * LANES : (b + 1) * LANES]
+                right = result[at, (b + 1) * LANES : (b + 2) * LANES]
+                both = jnp.concatenate([left, right], axis=0).astype(bf16)
+                out_ref[15 - d, p * (BLOCKS // 2) + b // 2] = both
         end = jnp.where(lane == p, sums[LANES:, BLOCKS * LANES :], end)
-    end = end.reshape(16, 8, LANES)
-    out_ref[:, pairs * (BLOCKS // 2)] = jnp.concatenate([end, end], axis=1).astype(bf16)
+    for d in range(16):
+        last = end[d * 8 : (d + 1) * 8]
+        out_ref[15 - d, pairs * (BLOCKS // 2)] = jnp.concatenate([last, last], axis=0).astype(bf16)
 
 
 def contract(order, buffer, back):
@@ -200,7 +206,7 @@
         stores.append(pltpu.make_async_copy(out_ref.at[:, part], out_hbm.at[:, part], sems.at[i]))
     for d in range(senders):
         rows = rows_ref.at[d % 2]
-        rows[...] = in_ref[d].astype(f32)
+        rows[...] = in_ref[senders - 1 - d].astype(f32)
         for p in range(pairs):
             for b in range(BLOCKS):
                 for l in range(4):
@@ -226,7 +232,7 @@
         scratch_shapes=[
             pltpu.VMEM((2, blocks, 16, LANES), f32),
             pltpu.VMEM(out.shape, f32),
-            pltpu.SemaphoreType.DMA((8,)),
+            pltpu.SemaphoreType.DMA((4,)),
         ],
         compiler_params=params(),
         name="unpack",
@@ -462,7 +468,9 @@
 
     def exchange_pairs(blocks):
         rows = blocks.reshape(lev_count, -1, LANES)
-        return lax.all_to_all(rows, "lev", 0, 0, tiled=True).reshape(blocks.shape)
+        backwards = [list(reversed(range(lev_count)))]
+        rows = lax.all_to_all(rows, "lev", 0, 0, tiled=True, axis_index_groups=backwards)
+        return rows.reshape(blocks.shape)
 
     def exchange_rows(rows):
         rows = rows.reshape(devices, pairs, 2, LANES).transpose(0, 2, 1, 3).reshape(devices, 2, -1)

time: 133 us -> 131 us (0.985)
  blocking collectives: 92.4 us -> 89.8 us
  Pallas kernels: 24.8 us -> 23.2 us
  starting transfers between devices: 8.25 us -> 9.85 us
    all_to_all x2, blocking collectives: 75.9 us -> 73.3 us  [exchange_pairs(): lax.all_to_all(rows, 'lev', 0, 0, tiled=True, axis_index_groups=backwards)]
    all_to_all x1, starting transfers between devices: 8.25 us -> 9.85 us  [exchange_rows(): lax.all_to_all(rows, ('lev', 'band'), 0, 0, tiled=True)]
where the time goes in v5:
time: 131 us; the launch traced here: 130 us
  blocking collectives  89.8 us (69%)
  Pallas kernels  23.2 us (18%)
  starting transfers between devices  9.85 us (8%)
  waiting for transfers between devices  4.91 us (4%)
  local copies, waits for them, and re-layouts  1.8 us (1%)
    all_to_all x2, blocking collectives, exchange_pairs(): lax.all_to_all(rows, 'lev', 0, 0, tiled=True, axis_index_groups=backwards)  73.3 us
    all_to_all x1, blocking collectives, exchange_rows(): lax.all_to_all(rows, ('lev', 'band'), 0, 0, tiled=True)  16.5 us
    all_to_all x1, starting transfers between devices, exchange_rows(): lax.all_to_all(rows, ('lev', 'band'), 0, 0, tiled=True)  9.85 us
    pallas_call x1, Pallas kernels, grid_step(): pl.pallas_call(grid_kernel, in_specs=[smem, smem, smem, vmem, pl.BlockSpe...  8.14 us
    pallas_call x1, Pallas kernels, basis(): pl.pallas_call(basis_kernel, grid=(pairs // rows,), in_specs=[pl.BlockSpe...  5.3 us
    all_to_all x1, waiting for transfers between devices, exchange_rows(): lax.all_to_all(rows, ('lev', 'band'), 0, 0, tiled=True)  4.91 us
    pallas_call x1, Pallas kernels, pack(): pl.pallas_call(pack_kernel, in_specs=[hbm, hbm], out_specs=hbm, out_shape...  3.47 us
  transfers between devices with their start and end apart: 1, of which 1 were waited for; matrix products, arithmetic and copies ran while one was open for 1% of the time, Pallas kernels for 4%

profile of v5, /device:TPU:0, one launch (start us, length us, event | category | flops | bytes accessed | tf_op | source)
XLA Modules:
  0.0 130.2 jit_solution(4855611057635225651)
XLA Ops:
  0.6 3.5 %pack.1 = bf16[16,51,16,128]{3,2,1,0:T(8,128)(2,1)} custom-call(bf16[80,8,1281]{2,1,0:T(8,128)(2,1)} %leg_hbm.1, bf16[4,80,2,1281]{3,2,1,0:T(2,128)(2,1)} %spec_hbm.1), custom_call_target="tpu_custom_call" | custom-call | tf_op jit(solution)/shard_map/pack/pallas_call | solution.py:91
  4.1 0.0 copy-start.1
  4.1 46.8 %all_to_all.20 = bf16[16,816,128]{2,1,0:T(8,128)(2,1)S(1)} all-to-all(bf16[16,816,128]{2,1,0:T(8,128)(2,1)} %bitcast.31), channel_id=1, replica_groups={{15,14,13,12,11,10,9,8,7,6,5,4,3,2,1,0},{31,30,29,28,27,26,25,24,23,22,..., dimensions={0} | all-to-all | bytes 6684672 | tf_op jit(solution)/shard_map/all_to_all | solution.py:472
  51.0 0.0 copy-done.1
  51.0 2.1 %invert.1 = bf16[1280,128]{1,0:T(8,128)(2,1)S(1)} custom-call(s32[640]{0:T(1024)S(1)} %copy-done.1, bf16[16,51,16,128]{3,2,1,0:T(8,128)(2,1)S(1)} %bitcast.25), custom_call_target="tpu_custom_call" | custom-call | tf_op jit(solution)/shard_map/invert/pallas_call | solution.py:143
  53.0 0.0 copy-start
  53.0 0.7 copy-done
  53.8 9.9 %all-to-all-start.1 = ((bf16[128,2,640]{2,1,0:T(2,128)(2,1)}), bf16[128,2,640]{2,1,0:T(2,128)(2,1)}, u32[]{:S(2)}, u32[]{:S(2)}) async-start(bf16[128,2,640]{2,1,0:T(2,128)(2,1)} %bitcast.30), calls=%async_computation.1 | async-start | bytes 655360 | tf_op jit(solution)/shard_map/all_to_all | solution.py:477
  63.6 0.2 reshape.48
  63.8 0.2 copy.8
  64.0 0.7 reshape.49.order_ref
  64.7 5.3 %basis.1.table_hbm = bf16[2,640,1408]{2,1,0:T(8,128)(2,1)} custom-call(s32[128]{0:T(128)} %row_lat_ref.1, s32[128]{0:T(128)} %lon_count_ref.1, s32[5,128]{1,0:T(8,128)} %reshape.49.order_ref), custom_call_target="tpu_custom_call" | custom-call | flops 200000000 | bytes 30000000 | tf_op jit(solution)/shard_map/basis/pallas_call | solution.py:290
  70.0 4.9 %all-to-all-done.1 = bf16[128,2,640]{2,1,0:T(2,128)(2,1)} async-done(((bf16[128,2,640]{2,1,0:T(2,128)(2,1)}), bf16[128,2,640]{2,1,0:T(2,128)(2,1)}, u32[]{:S(2)}, u32[]{:S(2)}) %all-to-all-start.1) | async-done | bytes 327712 | tf_op jit(solution)/shard_map/all_to_all | solution.py:477
  74.9 8.1 %grid.1 = (f32[64,1,5136]{2,1,0:T(1,128)}, bf16[1280,128]{1,0:T(8,128)(2,1)}) custom-call(s32[128]{0:T(128)} %row_lat_ref.1, s32[128]{0:T(128)} %lon_count_ref.1, f32[8]{0:T(128)} %weight_ref.1, s32[5,128]{1,0:T(8,128)} %reshape.49.order_ref, bf16[2,640,1408]{2,1,0:T(8,128)(2,1)} %basis.1.table_hbm, bf16[1280,128]{1,0:T(8,128)(2,1)} %bitcast.8.in_ref), custom_call_target="tpu_custom_call" | custom-call | tf_op jit(solution)/shard_map/grid/pallas_call | solution.py:442
  83.1 16.5 %all_to_all.21 = bf16[128,2,640]{2,1,0:T(2,128)(2,1)S(1)} all-to-all(bf16[128,2,640]{2,1,0:T(2,128)(2,1)} %bitcast.32), channel_id=1, replica_groups=mesh['band'=8,'lev'=16] {'lev','band'}, dimensions={0} | all-to-all | bytes 655360 | tf_op jit(solution)/shard_map/all_to_all | solution.py:477
  99.6 1.8 %contract.1 = bf16[16,26,16,128]{3,2,1,0:T(8,128)(2,1)S(1)} custom-call(s32[640]{0:T(1024)S(1)} %copy-done.1, bf16[16,51,16,128]{3,2,1,0:T(8,128)(2,1)S(1)} %bitcast.26, bf16[1280,128]{1,0:T(8,128)(2,1)S(1)} %bitcast.29), custom_call_target="tpu_custom_call" | custom-call | tf_op jit(solution)/shard_map/contract/pallas_call | solution.py:187
  101.4 26.5 %all_to_all.22 = bf16[16,416,128]{2,1,0:T(8,128)(2,1)S(1)} all-to-all(bf16[16,416,128]{2,1,0:T(8,128)(2,1)S(1)} %bitcast.27), channel_id=1, replica_groups={{15,14,13,12,11,10,9,8,7,6,5,4,3,2,1,0},{31,30,29,28,27,26,25,24,23,22,..., dimensions={0} | all-to-all | bytes 3407872 | tf_op jit(solution)/shard_map/all_to_all | solution.py:472
  127.9 2.3 %unpack.1 = f32[4,80,2,1281]{3,2,1,0:T(2,128)} custom-call(bf16[16,26,16,128]{3,2,1,0:T(8,128)(2,1)S(1)} %bitcast.28), custom_call_target="tpu_custom_call" | custom-call | tf_op jit(solution)/shard_map/unpack/pallas_call | solution.py:227
Async XLA Ops:
  4.1 46.9 %copy-start.1 = (s32[640]{0:T(1024)S(1)}, s32[640]{0:T(1024)}, u32[]{:S(2)}) copy-start(s32[640]{0:T(1024)} %order_ref.3) | copy-start | bytes 7684
  53.0 0.7 copy-start
  53.8 21.1 %all-to-all-start.1 = ((bf16[128,2,640]{2,1,0:T(2,128)(2,1)}), bf16[128,2,640]{2,1,0:T(2,128)(2,1)}, u32[]{:S(2)}, u32[]{:S(2)}) async-start(bf16[128,2,640]{2,1,0:T(2,128)(2,1)} %bitcast.30), calls=%async_computation.1 | async-start | bytes 655360 | tf_op jit(solution)/shard_map/all_to_all | solution.py:477

commit v6 on v5

--- a/solution.py
+++ b/solution.py
@@ -303,7 +303,9 @@
     )(row_lat, lon_count, order)
 
 
-def grid_kernel(row_lat_ref, lon_count_ref, weight_ref, order_ref, table_hbm, in_ref, grid_hbm, back_ref, place, rows_ref, table_ref, grid_ref, sems):
+def grid_kernel(row_lat_ref, lon_count_ref, weight_ref, order_ref, table_hbm, in_hbm, grid_hbm, back_ref, place, rows_ref, table_ref, grid_ref, in_ref, sems):
+    enter = pltpu.make_async_copy(in_hbm, in_ref, sems.at[3])
+    enter.start()
     loads = [pltpu.make_async_copy(table_hbm.at[i], table_ref.at[i], sems.at[i]) for i in range(2)]
     leave = pltpu.make_async_copy(grid_ref, grid_hbm, sems.at[2])
     for load in loads:
@@ -323,6 +325,7 @@
     sign_even = jnp.where(remainder(even, 4.0) < 0.5, 1.0, -1.0)
     keep_even = jnp.where(2.0 * even < length, jnp.where(even < 0.5, 1.0, 2.0), 0.0)
     keep_odd = jnp.where(2.0 * odd < length, 2.0, 0.0)
+    enter.wait()
     rows_ref[...] = in_ref[...].astype(f32)
 
     def arrived(s):
@@ -441,7 +444,7 @@
     vmem = pl.BlockSpec(memory_space=pltpu.VMEM)
     return pl.pallas_call(
         grid_kernel,
-        in_specs=[smem, smem, smem, vmem, pl.BlockSpec(memory_space=pltpu.HBM), vmem],
+        in_specs=[smem, smem, smem, vmem, pl.BlockSpec(memory_space=pltpu.HBM), pl.BlockSpec(memory_space=pl.ANY)],
         out_specs=[pl.BlockSpec(memory_space=pltpu.HBM), vmem],
         out_shape=[
             jax.ShapeDtypeStruct((64, 1, WIDTH), f32),
@@ -452,7 +455,8 @@
             pltpu.VMEM((rows, LANES), f32),
             pltpu.VMEM(table.shape, bf16),
             pltpu.VMEM((64, 1, WIDTH), f32),
-            pltpu.SemaphoreType.DMA((3,)),
+            pltpu.VMEM(coeffs.shape, bf16),
+            pltpu.SemaphoreType.DMA((4,)),
         ],
         compiler_params=params(60),
         name="grid",

time: 131 us -> 130 us (level)
  no operation moved by 1% of the time
where the time goes in v6:
time: 130 us
  blocking collectives  89.8 us (69%)
  Pallas kernels  23 us (18%)
  starting transfers between devices  9.85 us (8%)
  waiting for transfers between devices  4.91 us (4%)
  local copies, waits for them, and re-layouts  1.8 us (1%)
    all_to_all x2, blocking collectives, exchange_pairs(): lax.all_to_all(rows, 'lev', 0, 0, tiled=True, axis_index_groups=backwards)  73.3 us
    all_to_all x1, blocking collectives, exchange_rows(): lax.all_to_all(rows, ('lev', 'band'), 0, 0, tiled=True)  16.5 us
    all_to_all x1, starting transfers between devices, exchange_rows(): lax.all_to_all(rows, ('lev', 'band'), 0, 0, tiled=True)  9.85 us
    pallas_call x1, Pallas kernels, grid_step(): pl.pallas_call(grid_kernel, in_specs=[smem, smem, smem, vmem, pl.BlockSpe...  7.97 us
    pallas_call x1, Pallas kernels, basis(): pl.pallas_call(basis_kernel, grid=(pairs // rows,), in_specs=[pl.BlockSpe...  5.3 us
    all_to_all x1, waiting for transfers between devices, exchange_rows(): lax.all_to_all(rows, ('lev', 'band'), 0, 0, tiled=True)  4.91 us
    pallas_call x1, Pallas kernels, pack(): pl.pallas_call(pack_kernel, in_specs=[hbm, hbm], out_specs=hbm, out_shape...  3.47 us
  transfers between devices with their start and end apart: 1, of which 1 were waited for; matrix products, arithmetic and copies ran while one was open for 1% of the time, Pallas kernels for 4%

profile of v6, /device:TPU:0, one launch (start us, length us, event | category | flops | bytes accessed | tf_op | source)
XLA Modules:
  0.0 130.1 jit_solution(13392113678820778118)
XLA Ops:
  0.6 3.5 %pack.1 = bf16[16,51,16,128]{3,2,1,0:T(8,128)(2,1)} custom-call(bf16[80,8,1281]{2,1,0:T(8,128)(2,1)} %leg_hbm.1, bf16[4,80,2,1281]{3,2,1,0:T(2,128)(2,1)} %spec_hbm.1), custom_call_target="tpu_custom_call" | custom-call | tf_op jit(solution)/shard_map/pack/pallas_call | solution.py:91
  4.1 0.0 copy-start.1
  4.1 46.8 %all_to_all.20 = bf16[16,816,128]{2,1,0:T(8,128)(2,1)S(1)} all-to-all(bf16[16,816,128]{2,1,0:T(8,128)(2,1)} %bitcast.31), channel_id=1, replica_groups={{15,14,13,12,11,10,9,8,7,6,5,4,3,2,1,0},{31,30,29,28,27,26,25,24,23,22,..., dimensions={0} | all-to-all | bytes 6684672 | tf_op jit(solution)/shard_map/all_to_all | solution.py:476
  51.0 0.0 copy-done.1
  51.0 2.1 %invert.1 = bf16[1280,128]{1,0:T(8,128)(2,1)S(1)} custom-call(s32[640]{0:T(1024)S(1)} %copy-done.1, bf16[16,51,16,128]{3,2,1,0:T(8,128)(2,1)S(1)} %bitcast.25), custom_call_target="tpu_custom_call" | custom-call | tf_op jit(solution)/shard_map/invert/pallas_call | solution.py:143
  53.0 0.0 copy-start
  53.0 0.7 copy-done
  53.8 9.9 %all-to-all-start.1 = ((bf16[128,2,640]{2,1,0:T(2,128)(2,1)}), bf16[128,2,640]{2,1,0:T(2,128)(2,1)}, u32[]{:S(2)}, u32[]{:S(2)}) async-start(bf16[128,2,640]{2,1,0:T(2,128)(2,1)} %bitcast.30), calls=%async_computation.1 | async-start | bytes 655360 | tf_op jit(solution)/shard_map/all_to_all | solution.py:481
  63.6 0.2 reshape.48
  63.8 0.2 copy.8
  64.0 0.7 reshape.49.order_ref
  64.7 5.3 %basis.1.table_hbm = bf16[2,640,1408]{2,1,0:T(8,128)(2,1)} custom-call(s32[128]{0:T(128)} %row_lat_ref.1, s32[128]{0:T(128)} %lon_count_ref.1, s32[5,128]{1,0:T(8,128)} %reshape.49.order_ref), custom_call_target="tpu_custom_call" | custom-call | flops 200000000 | bytes 30000000 | tf_op jit(solution)/shard_map/basis/pallas_call | solution.py:290
  70.0 4.9 %all-to-all-done.1 = bf16[128,2,640]{2,1,0:T(2,128)(2,1)} async-done(((bf16[128,2,640]{2,1,0:T(2,128)(2,1)}), bf16[128,2,640]{2,1,0:T(2,128)(2,1)}, u32[]{:S(2)}, u32[]{:S(2)}) %all-to-all-start.1) | async-done | bytes 327712 | tf_op jit(solution)/shard_map/all_to_all | solution.py:481
  74.9 8.0 %grid.1 = (f32[64,1,5136]{2,1,0:T(1,128)}, bf16[1280,128]{1,0:T(8,128)(2,1)}) custom-call(s32[128]{0:T(128)} %row_lat_ref.1, s32[128]{0:T(128)} %lon_count_ref.1, f32[8]{0:T(128)} %weight_ref.1, s32[5,128]{1,0:T(8,128)} %reshape.49.order_ref, bf16[2,640,1408]{2,1,0:T(8,128)(2,1)} %basis.1.table_hbm, bf16[1280,128]{1,0:T(8,128)(2,1)} %bitcast.8.in_hbm), custom_call_target="tpu_custom_call" | custom-call | tf_op jit(solution)/shard_map/grid/pallas_call | solution.py:445
  82.9 16.5 %all_to_all.21 = bf16[128,2,640]{2,1,0:T(2,128)(2,1)S(1)} all-to-all(bf16[128,2,640]{2,1,0:T(2,128)(2,1)} %bitcast.32), channel_id=1, replica_groups=mesh['band'=8,'lev'=16] {'lev','band'}, dimensions={0} | all-to-all | bytes 655360 | tf_op jit(solution)/shard_map/all_to_all | solution.py:481
  99.4 1.8 %contract.1 = bf16[16,26,16,128]{3,2,1,0:T(8,128)(2,1)S(1)} custom-call(s32[640]{0:T(1024)S(1)} %copy-done.1, bf16[16,51,16,128]{3,2,1,0:T(8,128)(2,1)S(1)} %bitcast.26, bf16[1280,128]{1,0:T(8,128)(2,1)S(1)} %bitcast.29), custom_call_target="tpu_custom_call" | custom-call | tf_op jit(solution)/shard_map/contract/pallas_call | solution.py:187
  101.2 26.5 %all_to_all.22 = bf16[16,416,128]{2,1,0:T(8,128)(2,1)S(1)} all-to-all(bf16[16,416,128]{2,1,0:T(8,128)(2,1)S(1)} %bitcast.27), channel_id=1, replica_groups={{15,14,13,12,11,10,9,8,7,6,5,4,3,2,1,0},{31,30,29,28,27,26,25,24,23,22,..., dimensions={0} | all-to-all | bytes 3407872 | tf_op jit(solution)/shard_map/all_to_all | solution.py:476
  127.7 2.3 %unpack.1 = f32[4,80,2,1281]{3,2,1,0:T(2,128)} custom-call(bf16[16,26,16,128]{3,2,1,0:T(8,128)(2,1)S(1)} %bitcast.28), custom_call_target="tpu_custom_call" | custom-call | tf_op jit(solution)/shard_map/unpack/pallas_call | solution.py:227
Async XLA Ops:
  4.1 46.9 %copy-start.1 = (s32[640]{0:T(1024)S(1)}, s32[640]{0:T(1024)}, u32[]{:S(2)}) copy-start(s32[640]{0:T(1024)} %order_ref.3) | copy-start | bytes 7684
  53.0 0.7 copy-start
  53.8 21.1 %all-to-all-start.1 = ((bf16[128,2,640]{2,1,0:T(2,128)(2,1)}), bf16[128,2,640]{2,1,0:T(2,128)(2,1)}, u32[]{:S(2)}, u32[]{:S(2)}) async-start(bf16[128,2,640]{2,1,0:T(2,128)(2,1)} %bitcast.30), calls=%async_computation.1 | async-start | bytes 655360 | tf_op jit(solution)/shard_map/all_to_all | solution.py:481

commit v7 on v6

--- a/solution.py
+++ b/solution.py
@@ -199,25 +199,27 @@
     senders = in_ref.shape[0]
     pairs = out_ref.shape[1] // senders
     blocks = in_ref.shape[1]
-    steps = sems.shape[0]
-    stores = []
-    for i in range(steps):
-        part = pl.ds(i * (senders // steps) * pairs, (senders // steps) * pairs)
-        stores.append(pltpu.make_async_copy(out_ref.at[:, part], out_hbm.at[:, part], sems.at[i]))
+    ends = (6, 11, 14, senders)
+    stores = {}
+    for i, end in enumerate(ends):
+        start = ends[i - 1] if i else 0
+        part = pl.ds(start * pairs, (end - start) * pairs)
+        stores[end] = pltpu.make_async_copy(out_ref.at[:, part], out_hbm.at[:, part], sems.at[i])
     for d in range(senders):
         rows = rows_ref.at[d % 2]
         rows[...] = in_ref[senders - 1 - d].astype(f32)
+        tails = [rows[blocks - 1, pl.ds(0, 8), :][:, p : p + 1] for p in range(pairs)]
         for p in range(pairs):
             for b in range(BLOCKS):
                 for l in range(4):
                     pair = rows[p * (BLOCKS // 2) + b // 2, pl.ds(b % 2 * 8 + 2 * l, 2), :]
                     out_ref[l, d * pairs + p, :, b * LANES : (b + 1) * LANES] = pair
             for l in range(4):
-                last = rows[blocks - 1, pl.ds(2 * l, 2), :]
-                out_ref[l, d * pairs + p, :, COEFS - 1 : COEFS] = last[:, p : p + 1]
-        if (d + 1) % (senders // steps) == 0:
-            stores[d // (senders // steps)].start()
-    for store in stores:
+                last = tails[p][2 * l : 2 * l + 2]
+                out_ref[l, d * pairs + p, :, COEFS - 1 : COEFS] = last
+        if d + 1 in stores:
+            stores[d + 1].start()
+    for store in stores.values():
         store.wait()
 
 

time: 130 us -> 130 us (level)
  no operation moved by 1% of the time
where the time goes in v7:
time: 130 us
  blocking collectives  89.8 us (69%)
  Pallas kernels  23 us (18%)
  starting transfers between devices  9.85 us (8%)
  waiting for transfers between devices  4.91 us (4%)
  local copies, waits for them, and re-layouts  1.8 us (1%)
    all_to_all x2, blocking collectives, exchange_pairs(): lax.all_to_all(rows, 'lev', 0, 0, tiled=True, axis_index_groups=backwards)  73.3 us
    all_to_all x1, blocking collectives, exchange_rows(): lax.all_to_all(rows, ('lev', 'band'), 0, 0, tiled=True)  16.5 us
    all_to_all x1, starting transfers between devices, exchange_rows(): lax.all_to_all(rows, ('lev', 'band'), 0, 0, tiled=True)  9.85 us
    pallas_call x1, Pallas kernels, grid_step(): pl.pallas_call(grid_kernel, in_specs=[smem, smem, smem, vmem, pl.BlockSpe...  7.97 us
    pallas_call x1, Pallas kernels, basis(): pl.pallas_call(basis_kernel, grid=(pairs // rows,), in_specs=[pl.BlockSpe...  5.3 us
    all_to_all x1, waiting for transfers between devices, exchange_rows(): lax.all_to_all(rows, ('lev', 'band'), 0, 0, tiled=True)  4.91 us
    pallas_call x1, Pallas kernels, pack(): pl.pallas_call(pack_kernel, in_specs=[hbm, hbm], out_specs=hbm, out_shape...  3.47 us
  transfers between devices with their start and end apart: 1, of which 1 were waited for; matrix products, arithmetic and copies ran while one was open for 1% of the time, Pallas kernels for 4%

profile of v7, /device:TPU:0, one launch (start us, length us, event | category | flops | bytes accessed | tf_op | source)
XLA Modules:
  0.0 130.1 jit_solution(9875421828243397595)
XLA Ops:
  0.6 3.5 %pack.1 = bf16[16,51,16,128]{3,2,1,0:T(8,128)(2,1)} custom-call(bf16[80,8,1281]{2,1,0:T(8,128)(2,1)} %leg_hbm.1, bf16[4,80,2,1281]{3,2,1,0:T(2,128)(2,1)} %spec_hbm.1), custom_call_target="tpu_custom_call" | custom-call | tf_op jit(solution)/shard_map/pack/pallas_call | solution.py:91
  4.1 0.0 copy-start.1
  4.1 46.8 %all_to_all.20 = bf16[16,816,128]{2,1,0:T(8,128)(2,1)S(1)} all-to-all(bf16[16,816,128]{2,1,0:T(8,128)(2,1)} %bitcast.31), channel_id=1, replica_groups={{15,14,13,12,11,10,9,8,7,6,5,4,3,2,1,0},{31,30,29,28,27,26,25,24,23,22,..., dimensions={0} | all-to-all | bytes 6684672 | tf_op jit(solution)/shard_map/all_to_all | solution.py:478
  51.0 0.0 copy-done.1
  51.0 2.1 %invert.1 = bf16[1280,128]{1,0:T(8,128)(2,1)S(1)} custom-call(s32[640]{0:T(1024)S(1)} %copy-done.1, bf16[16,51,16,128]{3,2,1,0:T(8,128)(2,1)S(1)} %bitcast.25), custom_call_target="tpu_custom_call" | custom-call | tf_op jit(solution)/shard_map/invert/pallas_call | solution.py:143
  53.0 0.0 copy-start
  53.0 0.7 copy-done
  53.8 9.9 %all-to-all-start.1 = ((bf16[128,2,640]{2,1,0:T(2,128)(2,1)}), bf16[128,2,640]{2,1,0:T(2,128)(2,1)}, u32[]{:S(2)}, u32[]{:S(2)}) async-start(bf16[128,2,640]{2,1,0:T(2,128)(2,1)} %bitcast.30), calls=%async_computation.1 | async-start | bytes 655360 | tf_op jit(solution)/shard_map/all_to_all | solution.py:483
  63.6 0.2 reshape.48
  63.8 0.2 copy.8
  64.0 0.7 reshape.49.order_ref
  64.7 5.3 %basis.1.table_hbm = bf16[2,640,1408]{2,1,0:T(8,128)(2,1)} custom-call(s32[128]{0:T(128)} %row_lat_ref.1, s32[128]{0:T(128)} %lon_count_ref.1, s32[5,128]{1,0:T(8,128)} %reshape.49.order_ref), custom_call_target="tpu_custom_call" | custom-call | flops 200000000 | bytes 30000000 | tf_op jit(solution)/shard_map/basis/pallas_call | solution.py:292
  70.0 4.9 %all-to-all-done.1 = bf16[128,2,640]{2,1,0:T(2,128)(2,1)} async-done(((bf16[128,2,640]{2,1,0:T(2,128)(2,1)}), bf16[128,2,640]{2,1,0:T(2,128)(2,1)}, u32[]{:S(2)}, u32[]{:S(2)}) %all-to-all-start.1) | async-done | bytes 327712 | tf_op jit(solution)/shard_map/all_to_all | solution.py:483
  74.9 8.0 %grid.1 = (f32[64,1,5136]{2,1,0:T(1,128)}, bf16[1280,128]{1,0:T(8,128)(2,1)}) custom-call(s32[128]{0:T(128)} %row_lat_ref.1, s32[128]{0:T(128)} %lon_count_ref.1, f32[8]{0:T(128)} %weight_ref.1, s32[5,128]{1,0:T(8,128)} %reshape.49.order_ref, bf16[2,640,1408]{2,1,0:T(8,128)(2,1)} %basis.1.table_hbm, bf16[1280,128]{1,0:T(8,128)(2,1)} %bitcast.8.in_hbm), custom_call_target="tpu_custom_call" | custom-call | tf_op jit(solution)/shard_map/grid/pallas_call | solution.py:447
  82.9 16.5 %all_to_all.21 = bf16[128,2,640]{2,1,0:T(2,128)(2,1)S(1)} all-to-all(bf16[128,2,640]{2,1,0:T(2,128)(2,1)} %bitcast.32), channel_id=1, replica_groups=mesh['band'=8,'lev'=16] {'lev','band'}, dimensions={0} | all-to-all | bytes 655360 | tf_op jit(solution)/shard_map/all_to_all | solution.py:483
  99.4 1.8 %contract.1 = bf16[16,26,16,128]{3,2,1,0:T(8,128)(2,1)S(1)} custom-call(s32[640]{0:T(1024)S(1)} %copy-done.1, bf16[16,51,16,128]{3,2,1,0:T(8,128)(2,1)S(1)} %bitcast.26, bf16[1280,128]{1,0:T(8,128)(2,1)S(1)} %bitcast.29), custom_call_target="tpu_custom_call" | custom-call | tf_op jit(solution)/shard_map/contract/pallas_call | solution.py:187
  101.2 26.5 %all_to_all.22 = bf16[16,416,128]{2,1,0:T(8,128)(2,1)S(1)} all-to-all(bf16[16,416,128]{2,1,0:T(8,128)(2,1)S(1)} %bitcast.27), channel_id=1, replica_groups={{15,14,13,12,11,10,9,8,7,6,5,4,3,2,1,0},{31,30,29,28,27,26,25,24,23,22,..., dimensions={0} | all-to-all | bytes 3407872 | tf_op jit(solution)/shard_map/all_to_all | solution.py:478
  127.7 2.4 %unpack.1 = f32[4,80,2,1281]{3,2,1,0:T(2,128)} custom-call(bf16[16,26,16,128]{3,2,1,0:T(8,128)(2,1)S(1)} %bitcast.28), custom_call_target="tpu_custom_call" | custom-call | tf_op jit(solution)/shard_map/unpack/pallas_call | solution.py:229
Async XLA Ops:
  4.1 46.9 %copy-start.1 = (s32[640]{0:T(1024)S(1)}, s32[640]{0:T(1024)}, u32[]{:S(2)}) copy-start(s32[640]{0:T(1024)} %order_ref.3) | copy-start | bytes 7684
  53.0 0.7 copy-start
  53.8 21.1 %all-to-all-start.1 = ((bf16[128,2,640]{2,1,0:T(2,128)(2,1)}), bf16[128,2,640]{2,1,0:T(2,128)(2,1)}, u32[]{:S(2)}, u32[]{:S(2)}) async-start(bf16[128,2,640]{2,1,0:T(2,128)(2,1)} %bitcast.30), calls=%async_computation.1 | async-start | bytes 655360 | tf_op jit(solution)/shard_map/all_to_all | solution.py:483
